TPU v7x, 256 devices: a whole 4x4x8 slice. The times are simulated.
256 devices in a mesh: dp: 32 (over z, y), tensor: 8 (over x, core).
Axes of the slice: x: 4, y: 4, z: 8, core: 2. Of those that a mesh axis runs over, the one named last changes fastest.
Arguments:
- activations: bfloat16 [8192, 8192], P('dp'), may hold values from -6 to 6
- out_grads: bfloat16 [8192, 4096], P('dp', 'tensor'), may hold values from -0.25 to 0.25
- owner: int32 [8, 16], P('tensor'), may hold values from 0 to 31, as said below
- slot: int32 [8, 16], P('tensor'), may hold values from 0 to 1, as said below
- left_state: float32 [8, 32, 2, 512, 512], P('tensor', 'dp'), as said below
- right_state: float32 [8, 32, 2, 512, 512], P('tensor', 'dp'), as said below
Outputs:
- direction: bfloat16 [8192, 4096], P('dp', 'tensor')
- left_out: float32 [8, 32, 2, 512, 512], P('tensor', 'dp')
- right_out: float32 [8, 32, 2, 512, 512], P('tensor', 'dp')
Inputs may be any that keep to these rules, and one draw needn't show every extreme that they name: For each index of tensor, at most 2 blocks share an owner and some owner holds exactly 2; no two blocks share an owner and a slot. `slot`: together with owner, distinct for all blocks of one index of tensor. `left_state`: symmetric and diagonally dominant with positive diagonal. `right_state`: symmetric and diagonally dominant with positive diagonal.
All inputs are finite; a program needn't handle non-finite values.
Results may differ from a plain program's by a relative error of at most 0.025.
Values may be sent and summed in bfloat16 or wider, within the bound.
A program may use at most 128 MiB of HBM per device.

v0:
```python
import jax
import jax.numpy as jnp
from jax import lax
from jax.sharding import PartitionSpec as P

BLOCK_ORDER = 512
ITERS = 2
NBC = 1
NBLK = 16


BETA = 0.95


def matrix_multiply(left, right):
    return jnp.matmul(left, right, precision=lax.Precision.HIGHEST)


def inverse_root(mat):
    eye = jnp.eye(mat.shape[-1], dtype=jnp.float32)
    norm = jnp.sqrt(jnp.sum(mat * mat, axis=(-2, -1), keepdims=True))
    scale = 5.0 / (2.0 * norm)
    mat_m = mat * scale
    root = eye * scale**0.25
    for step in range(ITERS):
        step_m = 1.25 * eye - 0.25 * mat_m
        root = matrix_multiply(root, step_m)
        if step + 1 < ITERS:
            square = matrix_multiply(step_m, step_m)
            mat_m = matrix_multiply(matrix_multiply(square, square), mat_m)
    return root


def lookup(table, where_at):
    hits = where_at[..., None] == jnp.arange(table.shape[0], dtype=jnp.int32)
    return jnp.sum(jnp.where(hits, table, 0), axis=-1)


def send_back(blocks, owner_devices, owner_slots, count, device_self, rows, piece_rows, cols):
    spans = BLOCK_ORDER // piece_rows
    per_dev = rows // piece_rows * NBC
    out_pieces = blocks.reshape(blocks.shape[0] * spans, piece_rows, BLOCK_ORDER)
    dests = jnp.arange(count, dtype=jnp.int32)[:, None]
    pidx = jnp.arange(per_dev, dtype=jnp.int32)[None, :]
    grow = dests * rows + pidx // NBC * piece_rows
    blk = grow // BLOCK_ORDER * NBC + pidx % NBC
    span = grow % BLOCK_ORDER // piece_rows
    own = lookup(owner_devices, blk)
    held = lookup(owner_slots, blk)
    pick = jnp.take(out_pieces, (held * spans + span).reshape(-1), axis=0)
    pick = pick.reshape(count, per_dev, piece_rows, BLOCK_ORDER)
    outgoing = jnp.where((own == device_self)[:, :, None, None], pick, jnp.zeros((), jnp.bfloat16))
    incoming = lax.all_to_all(outgoing, "dp", split_axis=0, concat_axis=0, tiled=True)
    my_owner = lookup(
        owner_devices,
        (device_self * rows + pidx // NBC * piece_rows) // BLOCK_ORDER * NBC + pidx % NBC,
    )
    match = my_owner == dests
    back = jnp.sum(
        jnp.where(match[:, :, None, None], incoming, jnp.zeros((), jnp.bfloat16)), axis=0
    )
    back = back.reshape(rows // piece_rows, NBC, piece_rows, BLOCK_ORDER).transpose(0, 2, 1, 3)
    return back.reshape(rows, cols)


def shards(activations, out_grads, owner, slot, left_state, right_state):
    count = lax.axis_size("dp")
    device_self = lax.axis_index("dp")
    width = activations.shape[1]
    cols = out_grads.shape[1]
    rows = width // count
    piece_rows = min(rows, BLOCK_ORDER)
    spans = BLOCK_ORDER // piece_rows
    pieces_rows = rows // piece_rows
    per_dev = pieces_rows * NBC
    owner_devices = owner[0]
    owner_slots = slot[0]
    left_previous = left_state[0, 0]
    right_old = right_state[0, 0]
    slot_count = left_previous.shape[0]
    total = lax.psum_scatter(
        jnp.einsum("tr,tc->rc", activations, out_grads, preferred_element_type=jnp.float32).astype(
            jnp.bfloat16
        ),
        "dp",
        scatter_dimension=0,
        tiled=True,
    )
    grad_sq = jnp.sum(jnp.square(total.astype(jnp.float32)))
    owned_mask = (owner_devices[None, :] == device_self) & (
        owner_slots[None, :] == jnp.arange(slot_count, dtype=jnp.int32)[:, None]
    )
    used = jnp.any(owned_mask, axis=1)
    block_of = jnp.sum(jnp.where(owned_mask, jnp.arange(NBLK, dtype=jnp.int32)[None, :], 0), axis=1)
    block_row = block_of // NBC
    block_col = block_of % NBC
    pieces = total.reshape(pieces_rows, piece_rows, NBC, BLOCK_ORDER).transpose(0, 2, 1, 3)
    pieces = pieces.reshape(per_dev, piece_rows, BLOCK_ORDER)
    pidx = jnp.arange(per_dev, dtype=jnp.int32)
    first = device_self * rows + pidx // NBC * piece_rows
    dest = lookup(owner_devices, first // BLOCK_ORDER * NBC + pidx % NBC)
    onehot = dest[None, :] == jnp.arange(count, dtype=jnp.int32)[:, None]
    outgoing = jnp.where(onehot[:, :, None, None], pieces[None], jnp.zeros((), jnp.bfloat16))
    incoming = lax.all_to_all(outgoing, "dp", split_axis=0, concat_axis=0, tiled=True)
    flattened_blocks = incoming.reshape(count * per_dev, piece_rows, BLOCK_ORDER)
    global_row = (
        block_row[:, None] * BLOCK_ORDER + jnp.arange(spans, dtype=jnp.int32)[None, :] * piece_rows
    )
    block_index = (
        global_row // rows * per_dev + global_row % rows // piece_rows * NBC + block_col[:, None]
    )
    blocks = (
        jnp.take(flattened_blocks, block_index.reshape(-1), axis=0)
        .reshape(slot_count, BLOCK_ORDER, BLOCK_ORDER)
        .astype(jnp.float32)
    )
    gradient_blocks = jnp.where(used[:, None, None], blocks, 0.0)
    grads_low = gradient_blocks.astype(jnp.bfloat16)
    left_new = BETA * left_previous + jnp.einsum(
        "sij,skj->sik", grads_low, grads_low, preferred_element_type=jnp.float32
    )
    right_new = BETA * right_old + jnp.einsum(
        "sji,sjk->sik", grads_low, grads_low, preferred_element_type=jnp.float32
    )
    inverse_roots = inverse_root(jnp.concatenate([left_new, right_new], axis=0))
    preconditioned_update = matrix_multiply(
        matrix_multiply(inverse_roots[:slot_count], gradient_blocks), inverse_roots[slot_count:]
    )
    pre = jnp.where(used[:, None, None], preconditioned_update, 0.0).astype(jnp.bfloat16)
    kept = used[:, None, None]
    left_out = jnp.where(kept, left_new, left_previous)[None, None]
    right_out = jnp.where(kept, right_new, right_old)[None, None]
    pre_sq = jnp.sum(jnp.square(pre.astype(jnp.float32)))
    grad_total, pre_total = lax.psum((grad_sq, pre_sq), ("dp", "tensor"))
    ratio = jnp.sqrt(grad_total / pre_total)
    scaled = (lax.optimization_barrier(pre).astype(jnp.float32) * ratio).astype(jnp.bfloat16)
    direction = send_back(
        scaled, owner_devices, owner_slots, count, device_self, rows, piece_rows, cols
    )
    return (direction, left_out, right_out)


def solution(mesh):
    return jax.shard_map(
        shards,
        mesh=mesh,
        in_specs=(
            P("dp", None),
            P("dp", "tensor"),
            P("tensor", None),
            P("tensor", None),
            P("tensor", "dp", None, None, None),
            P("tensor", "dp", None, None, None),
        ),
        out_specs=(
            P("dp", "tensor"),
            P("tensor", "dp", None, None, None),
            P("tensor", "dp", None, None, None),
        ),
        check_vma=False,
    )
```

profile of v0, /device:TPU:1, one launch (start us, length us, event | category | flops | bytes accessed | tf_op | source)
XLA Modules:
  0.0 795.8 jit_solution(11247633495154219583)
XLA Ops:
  7.2 0.9 copy-done
  8.1 7.8 convolution_convert_fusion
  16.0 0.6 copy-done.6
  16.6 0.7 fusion.38
  17.2 0.6 iota_compare_fusion.2
  17.9 226.8 %reduce-scatter.2.cloned.1.call-done = bf16[256,512]{1,0:T(8,128)(2,1)} async-done(((bf16[8192,512]{1,0:T(8,128)(2,1)}), bf16[256,512]{1,0:T(8,128)(2,1)}) %reduce-scatter.2.cloned.1.call-update) | async-done | bytes 262160 | tf_op jit(solution)/shard_map/reduce_scatter | solution.py:81
  244.7 4.8 broadcast_select_fusion
  249.5 7.2 all-to-all-start
  257.6 1.1 fusion.32
  258.8 0.7 multiply_reduce_fusion.2
  259.5 177.0 %all-to-all-done = bf16[32,1,256,512]{3,2,1,0:T(8,128)(2,1)} async-done(((bf16[32,1,256,512]{3,2,1,0:T(8,128)(2,1)}), bf16[32,1,256,512]{3,2,1,0:T(8,128)(2,1)}, u32[]{:S(2)}, u32[]{:S(2)}) %all-to-all-start) | async-done | bytes 8388640 | tf_op jit(solution)/shard_map/all_to_all | solution.py:104
  436.5 4.0 gather_fusion
  440.5 0.2 bitcast_select_fusion.3
  440.7 2.6 fusion.11
  443.3 0.8 fusion.13
  444.1 0.5 multiply_reduce_fusion
  444.6 8.1 %fusion.8 = f32[4,512,512]{2,1,0:T(8,128)S(1)} fusion(f32[4]{0:T(128)S(1)} %get-tuple-element.10, f32[512,512]{1,0:T(8,128)S(1)} %fusion.31, f32[2,512,512]{2,1,0:T(8,128)S(1)} %fusion.11, f32[2,512,512]{2,1,0:T(8,128)S(1)} %fusion.13), kind=kOutput, calls=%fused_computation.17 | convolution fusion | flops 6446645248 | bytes 9437200 | tf_op jit(solution)/shard_map/dot_general | solution.py:16
  452.8 7.6 fusion.52
  460.4 7.6 fusion.6
  468.0 8.4 %fusion.4 = f32[4,512,512]{2,1,0:T(8,128)S(1)} fusion(f32[4]{0:T(128)S(1)} %get-tuple-element.10, f32[512,512]{1,0:T(8,128)S(1)} %fusion.31, f32[4]{0:T(128)S(1)} %get-tuple-element.9, f32[512,512]{1,0:T(8,128)S(1)} %copy-done.5, f32[2,512,512]{2,1,0:T(8,128)S(1)} %fusion.11, f32[2,512,512]{2,1,0:T(8,128)S(1)} %fusion.13), kind=kOutput, calls=%fused_computation.12 | convolution fusion | flops 6447693824 | bytes 10485792 | tf_op jit(solution)/shard_map/dot_general | solution.py:16
  476.4 7.9 fusion.1
  484.3 3.9 fusion.25
  488.2 5.1 multiply_reduce_fusion.1
  493.3 80.0 %all-reduce = (f32[]{:T(128)}, f32[]{:T(128)}) all-reduce(f32[]{:T(128)} %multiply_reduce_fusion.2, f32[]{:T(128)} %get-tuple-element.13), channel_id=1, replica_groups=mesh['dp'=32,'tensor'=8] {'dp','tensor'}, use_global_device_ids=true, to_apply=%region_9.10 | all-reduce | flops 2 | bytes 16 | tf_op jit(solution)/shard_map/psum | solution.py:134
  574.6 1.4 multiply_convert_fusion
  576.0 4.9 gather_fusion.1
  580.9 7.6 fusion
  588.4 7.1 all-to-all-start.1
  595.5 0.6 iota_compare_fusion.3
  596.2 6.0 fusion.12
  602.1 180.8 %all-to-all-done.1 = bf16[32,1,256,512]{3,2,1,0:T(8,128)(2,1)} async-done(((bf16[32,1,256,512]{3,2,1,0:T(8,128)(2,1)}), bf16[32,1,256,512]{3,2,1,0:T(8,128)(2,1)}, u32[]{:S(2)}, u32[]{:S(2)}) %all-to-all-start.1) | async-done | bytes 8388640 | tf_op jit(solution)/shard_map/all_to_all | solution.py:53
  782.9 5.9 select_reduce_fusion
  (34 shorter events, 1.0 us)
Async XLA Ops:
  7.2 1.0 copy-start
  7.2 237.5 %reduce-scatter.2.cloned.1.call-start = ((), (), s32[]{:S(2)}) async-start(), calls=%async_computation.3 | async-start | bytes 8650752 | tf_op jit(solution)/shard_map/reduce_scatter | solution.py:81
  15.9 0.7 copy-start.6
  249.5 7.3 copy-start.7
  249.5 9.3 %copy-start.4 = (bf16[256,512]{1,0:T(8,128)(2,1)S(1)}, bf16[256,512]{1,0:T(8,128)(2,1)}, u32[]{:S(2)}) copy-start(bf16[256,512]{1,0:T(8,128)(2,1)} %reduce-scatter.2.cloned.1.call-done) | copy-start | bytes 786436
  249.5 187.0 %all-to-all-start = ((bf16[32,1,256,512]{3,2,1,0:T(8,128)(2,1)}), bf16[32,1,256,512]{3,2,1,0:T(8,128)(2,1)}, u32[]{:S(2)}, u32[]{:S(2)}) async-start(bf16[32,1,256,512]{3,2,1,0:T(8,128)(2,1)} %broadcast_select_fusion), calls=%async_computation.1 | async-start | bytes 16777216 | tf_op jit(solution)/shard_map/all_to_all | solution.py:104
  440.5 2.8 copy-start.3
  444.1 23.9 %copy-start.2 = (f32[2,512,512]{2,1,0:T(8,128)}, f32[2,512,512]{2,1,0:T(8,128)S(1)}, u32[]{:S(2)}) copy-start(f32[2,512,512]{2,1,0:T(8,128)S(1)} %fusion.13) | copy-start | bytes 6291460
  460.4 7.6 copy-start.5
  588.4 194.5 %all-to-all-start.1 = ((bf16[32,1,256,512]{3,2,1,0:T(8,128)(2,1)}), bf16[32,1,256,512]{3,2,1,0:T(8,128)(2,1)}, u32[]{:S(2)}, u32[]{:S(2)}) async-start(bf16[32,1,256,512]{3,2,1,0:T(8,128)(2,1)} %fusion), calls=%async_computation.2 | async-start | bytes 16777216 | tf_op jit(solution)/shard_map/all_to_all | solution.py:53
  596.1 192.6 %copy-start.1 = (bf16[256,512]{1,0:T(8,128)(2,1)S(1)}, bf16[256,512]{1,0:T(8,128)(2,1)}, u32[]{:S(2)}) copy-start(bf16[256,512]{1,0:T(8,128)(2,1)} %param.7) | copy-start | bytes 786436
Sparse Core Ops, SparseCore 0:
  16.1 228.5 reduce-scatter.1
where the time goes:
time: 806 us; the launch traced here: 796 us
  waiting for transfers between devices  585 us (73%)
  blocking collectives  80 us (10%)
  matrix products  59.8 us (7%)
  other arithmetic  30.8 us (4%)
  between operations  15.8 us (2%)
  starting transfers between devices  14.3 us (2%)
  local copies, waits for them, and re-layouts  10.6 us (1%)
    reduce_scatter x1, waiting for transfers between devices, shards(): lax.psum_scatter(jnp.einsum('tr,tc->rc', activations, out_grads, preferre...  227 us
    all_to_all x1, waiting for transfers between devices, send_back(): lax.all_to_all(outgoing, 'dp', split_axis=0, concat_axis=0, tiled=True)  181 us
    all_to_all x1, waiting for transfers between devices, shards(): lax.all_to_all(outgoing, 'dp', split_axis=0, concat_axis=0, tiled=True)  177 us
    psum x1, blocking collectives, shards(): grad_total, pre_total = lax.psum((grad_sq, pre_sq), ('dp', 'tensor'))  80 us
    dot_general x7, matrix products, matrix_multiply(): return jnp.matmul(left, right, precision=lax.Precision.HIGHEST)  48.6 us
  transfers between devices with their start and end apart: 3, of which 3 were waited for; matrix products, arithmetic and copies ran while one was open for 1% of the time, Pallas kernels for 0%

commit v1 on v0

v1 whole, which is shorter than its diff:
```python
import functools

import jax
import jax.numpy as jnp
from jax import lax
from jax.experimental import pallas as pl
from jax.experimental.pallas import tpu as pltpu
from jax.sharding import PartitionSpec as P

N = 512
Q = 128
NZ, NY, NT = 8, 4, 8
SLOTS, NBLK, TOK = 2, 16, 256
BETA = 0.95
MESH = pl.DeviceIdType.MESH
RIGHT, LEFT = 0, 1
bf16, f32 = jnp.bfloat16, jnp.float32


def place():
    dp, t = lax.axis_index("dp"), lax.axis_index("tensor")
    return dp, t, dp // NY, lax.rem(dp, NY)


def ring(z, step):
    return lax.rem(z + step + NZ, NZ)


def remote(src, dst, send, recv, dp, t):
    return pltpu.make_async_remote_copy(
        src_ref=src, dst_ref=dst, send_sem=send, recv_sem=recv,
        device_id=(dp, t), device_id_type=MESH,
    )


def dot(a, b, ca, cb):
    return lax.dot_general(a, b, (((ca,), (cb,)), ((), ())), preferred_element_type=f32)


def barrier(peers):
    sem = pltpu.get_barrier_semaphore()
    for dp, t in peers:
        pl.semaphore_signal(sem, inc=1, device_id=(dp, t), device_id_type=MESH)
    pl.semaphore_wait(sem, len(peers))


def held(own_ref, slot_ref, device, slot):
    block, used = jnp.int32(0), jnp.int32(0)
    for b in range(NBLK):
        hit = (own_ref[b] == device) & (slot_ref[b] == slot)
        block = jnp.where(hit, b, block)
        used = jnp.where(hit, 1, used)
    return block, used


def chunk_of(z, k):
    far = 4 - (k + 1) // 2
    return ring(z, far if k % 2 else -far)


def grads_kernel(
    a_ref, o_ref, own_ref, slot_ref, h_ref,
    a_buf, ot_buf, snd, rcv, gath, stage,
    o_send, o_recv, own_sem, a_send, a_recv, f_send, f_recv,
    r_send, r_recv, g_send, g_recv, y_send, y_recv,
):
    dp, t, z, y = place()
    core = lax.rem(t, 2)
    twin = t + 1 - 2 * core
    ys = [lax.rem(y + j, NY) for j in range(NY)]
    ydp = [z * NY + yj for yj in ys]
    side = [ring(z, 1) * NY + y, ring(z, -1) * NY + y]
    barrier([(ydp[1], t), (ydp[2], t), (ydp[3], t), (side[0], t), (side[1], t), (dp, twin)])

    def columns(c, p, yj):
        return a_ref.at[:, pl.ds(pl.multiple_of((2 * c + p) * N + yj * Q, Q), Q)]

    def a_part(c, p, src):
        return a_buf.at[c, p, pl.ds(pl.multiple_of(src * TOK, TOK), TOK)]

    ot_buf[y] = o_ref[...].T
    waits = []

    def o_copy(j, src):
        return remote(ot_buf.at[src], ot_buf.at[src], o_send.at[j], o_recv.at[j], ydp[j], t)

    for j in (1, 3, 2):
        o_copy(j, y).start()

    def a_copy(k, j, src):
        c = chunk_of(z, k)
        return remote(
            columns(c, core, ys[j]), a_part(c, core, src),
            a_send.at[k, j], a_recv.at[k, j], ydp[j], t,
        )

    def own_copy(k, p):
        c = chunk_of(z, k)
        return pltpu.make_async_copy(columns(c, p, y), a_part(c, p, y), own_sem.at[k, p])

    for k in range(NZ):
        for j in (2, 1, 3):
            a_copy(k, j, y).start()
        for p in range(2):
            own_copy(k, p).start()

    def f_copy(k, j, p):
        part = a_part(chunk_of(z, k), p, ys[(NY - j) % NY])
        return remote(part, part, f_send.at[k, j], f_recv.at[k, j], dp, twin)

    def forward(k):
        for j in (1, 3, 2):
            a_copy(k, j, ys[(NY - j) % NY]).wait_recv()
            f_copy(k, j, core).start()

    def chain(d, s, p, to):
        return remote(snd.at[d, s, p], rcv.at[d, s, p], r_send.at[d, s, p], r_recv.at[d, s, p], to, t)

    forward(0)
    for j in (1, 3, 2):
        o_copy(j, ys[(NY - j) % NY]).wait_recv()
    sent = []
    for k in range(NZ):
        c = chunk_of(z, k)
        if k + 1 < NZ:
            forward(k + 1)
        for p in range(2):
            own_copy(k, p).wait()
        for j in (1, 3, 2):
            f_copy(k, j, 1 - core).wait_recv()
        acts = jnp.concatenate([a_buf[c, 0], a_buf[c, 1]], axis=1)
        outs = jnp.concatenate([ot_buf[j] for j in range(NY)], axis=1)
        part = dot(outs, acts, 1, 0)
        part = [part[:, :Q], part[:, Q:]]
        if k == 0:
            moves = [(RIGHT, 0, 0), (LEFT, 0, 1)]
        elif k < NZ - 1:
            moves = [((RIGHT if k % 2 else LEFT), (k + 1) // 2, p) for p in range(2)]
        else:
            moves = []
        for d, s, p in moves:
            value = part[p]
            if s > 1 or (s == 1 and p == d):
                chain(d, s - 1, p, side[d]).wait_recv()
                value = value + rcv[d, s - 1, p].astype(f32)
            snd[d, s, p] = value.astype(bf16)
            chain(d, s, p, side[d]).start()
            sent.append((d, s, p))
        if k == NZ - 1:
            for p in range(2):
                for d in (RIGHT, LEFT):
                    chain(d, 3, p, side[d]).wait_recv()
                total = part[p] + rcv[RIGHT, 3, p].astype(f32) + rcv[LEFT, 3, p].astype(f32)
                gath[2 * z + p] = total.astype(bf16)

    def g_copy(d, s, p):
        piece = gath.at[2 * ring(z, -s if d == RIGHT else s) + p]
        return remote(piece, piece, g_send.at[d, s, p], g_recv.at[d, s, p], side[d], t)

    def g_wait(d, s, p):
        piece = gath.at[2 * ring(z, -s - 1 if d == RIGHT else s + 1) + p]
        remote(piece, piece, g_send.at[d, s, p], g_recv.at[d, s, p], side[d], t).wait_recv()

    hops = [(s, p, d) for s in range(4) for p in range(2) for d in (RIGHT, LEFT) if s < 3 or p == d]
    for s, p, d in hops:
        if s > 0:
            g_wait(d, s - 1, p)
        g_copy(d, s, p).start()
    for d in (RIGHT, LEFT):
        g_wait(d, 2, 1 - d)
        g_wait(d, 3, d)

    def y_copy(j, src):
        return remote(stage.at[j], h_ref.at[src], y_send.at[j], y_recv.at[j], ydp[j], t)

    for j in (2, 1, 3, 0):
        for s in range(SLOTS):
            block, _ = held(own_ref, slot_ref, ydp[j], s)
            if j:
                stage[j, s] = gath[block]
            else:
                h_ref[y, s] = gath[block]
        if j:
            y_copy(j, y).start()
    for j in (1, 3, 2):
        y_copy(j, ys[(NY - j) % NY]).wait_recv()

    for j in (1, 2, 3):
        o_copy(j, y).wait_send()
        y_copy(j, y).wait_send()
        for k in range(NZ):
            a_copy(k, j, y).wait_send()
            f_copy(k, j, core).wait_send()
    for d, s, p in sent:
        chain(d, s, p, side[d]).wait_send()
    for s, p, d in hops:
        g_copy(d, s, p).wait_send()


def root(mat, eye):
    norm = jnp.sqrt(jnp.sum(mat * mat, axis=(0, 1), keepdims=True))
    scale = 2.5 / norm
    m = mat * scale
    mb = m.astype(bf16)
    square = dot(mb, mb, 1, 0)
    s2 = (1.5625 * eye - 0.625 * m + 0.0625 * square).astype(bf16)
    sm = (1.25 * m - 0.25 * square).astype(bf16)
    s4 = dot(s2, s2, 1, 0).astype(bf16)
    x = 1.5625 * eye - 0.3125 * m - 0.25 * dot(s4, sm, 1, 0)
    return (x * jnp.sqrt(jnp.sqrt(scale))).astype(bf16)


def update_kernel(used_ref, h_ref, l_ref, r_ref, lo_ref, ro_ref, p_ref, sum_ref):
    used = used_ref[pl.program_id(0)]

    @pl.when(used == 0)
    def _():
        lo_ref[...] = l_ref[...]
        ro_ref[...] = r_ref[...]
        p_ref[...] = jnp.zeros_like(p_ref)
        sum_ref[...] = jnp.zeros_like(sum_ref)

    @pl.when(used != 0)
    def _():
        h = jnp.concatenate([h_ref[j, 0] for j in range(NY)], axis=1)
        left = BETA * l_ref[0] + dot(h, h, 0, 0)
        lo_ref[0] = left
        right = BETA * r_ref[0] + dot(h, h, 1, 1)
        ro_ref[0] = right
        eye = (
            lax.broadcasted_iota(jnp.int32, (N, N), 0) == lax.broadcasted_iota(jnp.int32, (N, N), 1)
        ).astype(f32)
        part = dot(root(right, eye), h, 1, 0).astype(bf16)
        pre = dot(root(left, eye), part, 1, 1).astype(bf16)
        p_ref[0] = pre
        hf, pf = h.astype(f32), pre.astype(f32)
        sum_ref[0, 0] = jnp.broadcast_to(jnp.sum(hf * hf, axis=(0, 1), keepdims=True), (8, 128))
        sum_ref[0, 1] = jnp.broadcast_to(jnp.sum(pf * pf, axis=(0, 1), keepdims=True), (8, 128))


def back_kernel(
    p_ref, sum_ref, own_ref, slot_ref, out_ref,
    got, snd, rcv, mine, last, sums,
    y_send, y_recv, r_send, r_recv, l_send, l_recv, s_send, s_recv,
):
    dp, t, z, y = place()
    ys = [lax.rem(y + j, NY) for j in range(NY)]
    ydp = [z * NY + yj for yj in ys]
    side = [ring(z, 1) * NY + y, ring(z, -1) * NY + y]
    ts = [lax.rem(t + j, NT) for j in range(NT)]
    zdp = [ring(z, j) * NY + y for j in range(NZ)]
    barrier(
        [(ydp[j], t) for j in range(1, NY)]
        + [(dp, ts[j]) for j in range(1, NT)]
        + [(zdp[j], t) for j in range(1, NZ)]
    )

    def y_copy(j, src):
        rows = pl.ds(pl.multiple_of(ys[j] * Q, Q), Q)
        return remote(p_ref.at[:, rows], got.at[src], y_send.at[j], y_recv.at[j], ydp[j], t)

    for j in (2, 1, 3):
        y_copy(j, y).start()

    stages = [
        (NT, lambda j: (dp, ts[j])),
        (NY, lambda j: (ydp[j], t)),
        (NZ, lambda j: (zdp[j], t)),
    ]

    def s_copy(i, j):
        return remote(
            sums.at[i, 0], sums.at[i, j], s_send.at[i, j], s_recv.at[i, j], *stages[i][1](j)
        )

    def sum_start(i, value):
        sums[i, 0] = value
        for j in range(1, stages[i][0]):
            s_copy(i, j).start()

    def sum_end(i):
        for j in range(1, stages[i][0]):
            s_copy(i, j).wait_recv()
        return functools.reduce(jnp.add, [sums[i, j] for j in range(stages[i][0])])

    sum_start(0, sum_ref[0] + sum_ref[1])
    got[y] = p_ref[:, pl.ds(pl.multiple_of(y * Q, Q), Q)]
    sum_start(1, sum_end(0))
    for j in (1, 3, 2):
        y_copy(j, ys[(NY - j) % NY]).wait_recv()

    def chain(d, s, p, to):
        return remote(snd.at[d, s, p], rcv.at[d, s, p], r_send.at[d, s, p], r_recv.at[d, s, p], to, t)

    def place_of(c, p):
        b = 2 * c + p
        owner = own_ref[b]
        return owner // NY, lax.rem(owner, NY), slot_ref[b]

    sent = []
    for s in range(4):
        for p in range(2):
            for d in (RIGHT, LEFT):
                if s == 0 and p != d:
                    continue
                oz, oy, os = place_of(ring(z, 4 - s if d == RIGHT else s - 4), p)
                value = got[oy, os]
                if s > 1 or (s == 1 and p == d):
                    chain(d, s - 1, p, side[d]).wait_recv()
                    value = jnp.where(oz == z, value, rcv[d, s - 1, p])
                snd[d, s, p] = value
                chain(d, s, p, side[d]).start()
                sent.append((d, s, p))
        if s == 1:
            sum_start(2, sum_end(1))
    total = sum_end(2)
    ratio = jnp.sqrt(total[0] / total[1])[0:1, 0:1]
    for p in range(2):
        oz, oy, os = place_of(z, p)
        for d in (RIGHT, LEFT):
            chain(d, 3, p, side[d]).wait_recv()
        behind = ring(z, -oz)
        from_left = (behind < 4) | ((behind == 4) & (p == 0))
        value = jnp.where(from_left, rcv[RIGHT, 3, p], rcv[LEFT, 3, p])
        value = jnp.where(oz == z, got[oy, os], value)
        mine[p] = (value.astype(f32) * ratio).astype(bf16)

    def l_copy(p):
        return remote(
            mine.at[p], last.at[lax.rem(y, 2)], l_send.at[p], l_recv.at[lax.rem(y, 2)],
            z * NY + 2 * p + y // 2, t,
        )

    for p in range(2):
        to = 2 * p + y // 2

        @pl.when(to != y)
        def _():
            l_copy(p).start()

        @pl.when(to == y)
        def _():
            last[lax.rem(y, 2)] = mine[p]

    for q in range(2):
        src = 2 * lax.rem(y, 2) + q

        @pl.when(src != y)
        def _():
            remote(
                mine.at[0], last.at[q], l_send.at[0], l_recv.at[q], z * NY + src, t
            ).wait_recv()

        out_ref[pl.ds(q * Q, Q)] = last[q]

    for p in range(2):
        @pl.when(2 * p + y // 2 != y)
        def _():
            l_copy(p).wait_send()
    for j in range(1, NY):
        y_copy(j, y).wait_send()
    for i in range(3):
        for j in range(1, stages[i][0]):
            s_copy(i, j).wait_send()
    for d, s, p in sent:
        chain(d, s, p, side[d]).wait_send()


VMEM = pl.BlockSpec(memory_space=pltpu.VMEM)
SMEM = pl.BlockSpec(memory_space=pltpu.SMEM)
ANY = pl.BlockSpec(memory_space=pl.ANY)
DMA = pltpu.SemaphoreType.DMA


def shards(activations, out_grads, owner, slot, left_state, right_state):
    own, where = owner[0], slot[0]
    h = pl.pallas_call(
        grads_kernel,
        out_shape=jax.ShapeDtypeStruct((NY, SLOTS, N, Q), bf16),
        in_specs=[ANY, VMEM, SMEM, SMEM],
        out_specs=VMEM,
        scratch_shapes=[
            pltpu.VMEM((NZ, 2, NY * TOK, Q), bf16),
            pltpu.VMEM((NY, N, TOK), bf16),
            pltpu.VMEM((2, 4, 2, N, Q), bf16),
            pltpu.VMEM((2, 4, 2, N, Q), bf16),
            pltpu.VMEM((NBLK, N, Q), bf16),
            pltpu.VMEM((NY, SLOTS, N, Q), bf16),
            DMA((NY,)), DMA((NY,)), DMA((NZ, 2)), DMA((NZ, NY)), DMA((NZ, NY)),
            DMA((NZ, NY)), DMA((NZ, NY)), DMA((2, 4, 2)), DMA((2, 4, 2)),
            DMA((2, 4, 2)), DMA((2, 4, 2)), DMA((NY,)), DMA((NY,)),
        ],
        compiler_params=pltpu.CompilerParams(
            collective_id=0, has_side_effects=True, vmem_limit_bytes=40 * 2**20
        ),
        name="grads",
    )(activations, out_grads, own, where)

    me = lax.axis_index("dp")
    used = jnp.any(
        (own[None] == me) & (where[None] == jnp.arange(SLOTS, dtype=jnp.int32)[:, None]), axis=1
    ).astype(jnp.int32)
    state = pl.BlockSpec((1, N, N), lambda s: (s, 0, 0))
    left_out, right_out, pre, sums = pl.pallas_call(
        update_kernel,
        grid=(SLOTS,),
        out_shape=[
            jax.ShapeDtypeStruct((SLOTS, N, N), f32),
            jax.ShapeDtypeStruct((SLOTS, N, N), f32),
            jax.ShapeDtypeStruct((SLOTS, N, N), bf16),
            jax.ShapeDtypeStruct((SLOTS, 2, 8, 128), f32),
        ],
        in_specs=[SMEM, pl.BlockSpec((NY, 1, N, Q), lambda s: (0, s, 0, 0)), state, state],
        out_specs=[state, state, state, pl.BlockSpec((1, 2, 8, 128), lambda s: (s, 0, 0, 0))],
        compiler_params=pltpu.CompilerParams(vmem_limit_bytes=40 * 2**20),
        name="update",
    )(used, h, left_state[0, 0], right_state[0, 0])

    direction = pl.pallas_call(
        back_kernel,
        out_shape=jax.ShapeDtypeStruct((TOK, N), bf16),
        in_specs=[VMEM, VMEM, SMEM, SMEM],
        out_specs=VMEM,
        scratch_shapes=[
            pltpu.VMEM((NY, SLOTS, Q, N), bf16),
            pltpu.VMEM((2, 4, 2, Q, N), bf16),
            pltpu.VMEM((2, 4, 2, Q, N), bf16),
            pltpu.VMEM((2, Q, N), bf16),
            pltpu.VMEM((2, Q, N), bf16),
            pltpu.VMEM((3, NT, 2, 8, 128), f32),
            DMA((NY,)), DMA((NY,)), DMA((2, 4, 2)), DMA((2, 4, 2)),
            DMA((2,)), DMA((2,)), DMA((3, NT)), DMA((3, NT)),
        ],
        compiler_params=pltpu.CompilerParams(
            collective_id=1, has_side_effects=True, vmem_limit_bytes=40 * 2**20
        ),
        name="back",
    )(pre, sums, own, where)
    return direction, left_out[None, None], right_out[None, None]


def solution(mesh):
    return jax.shard_map(
        shards,
        mesh=mesh,
        in_specs=(
            P("dp", None),
            P("dp", "tensor"),
            P("tensor", None),
            P("tensor", None),
            P("tensor", "dp", None, None, None),
            P("tensor", "dp", None, None, None),
        ),
        out_specs=(
            P("dp", "tensor"),
            P("tensor", "dp", None, None, None),
            P("tensor", "dp", None, None, None),
        ),
        check_vma=False,
    )
```

time: 806 us -> 153 us (0.19)
  the two profiles are of different devices: /device:TPU:1 before, /device:TPU:8 now
where the time goes in v1:
time: 153 us
  Pallas kernels  146 us (95%)
  local copies, waits for them, and re-layouts  5.15 us (3%)
    pallas_call x1, Pallas kernels, shards(): pl.pallas_call(grads_kernel, out_shape=jax.ShapeDtypeStruct((NY, SLOTS, N...  86.9 us
    pallas_call x1, Pallas kernels, shards(): pl.pallas_call(back_kernel, out_shape=jax.ShapeDtypeStruct((TOK, N), bf16...  52.5 us
    pallas_call x1, Pallas kernels, shards(): pl.pallas_call(update_kernel, grid=(SLOTS,), out_shape=[jax.ShapeDtypeStr...  6.6 us
    unnamed x13, local copies, waits for them, and re-layouts  5.15 us

profile of v1, /device:TPU:8, one launch (start us, length us, event | category | flops | bytes accessed | tf_op | source)
XLA Modules:
  0.0 153.2 jit_solution(17639726787522230776)
XLA Ops:
  0.6 0.7 compare_bitcast_fusion
  1.3 0.8 and_reduce_fusion
  2.1 0.0 copy-start
  2.1 2.2 %copy-done = bf16[256,8192]{1,0:T(8,128)(2,1)S(1)} copy-done((bf16[256,8192]{1,0:T(8,128)(2,1)S(1)}, bf16[256,8192]{1,0:T(8,128)(2,1)}, u32[]{:S(2)}) %copy-start) | copy-done | bytes 4194328
  4.3 0.0 copy-start.3
  4.3 0.9 copy-done.3
  5.2 0.0 copy-start.4
  5.2 0.7 copy-done.4
  5.9 0.0 copy-start.5
  5.9 0.7 copy-done.5
  6.5 0.0 copy-start.1
  6.5 0.0 copy-start.2
  6.5 86.9 %grads.1.h_ref = bf16[4,2,512,128]{3,2,1,0:T(8,128)(2,1)S(1)} custom-call(bf16[256,8192]{1,0:T(8,128)(2,1)S(1)} %copy-done, bf16[256,512]{1,0:T(8,128)(2,1)S(1)} %copy-done.3, s32[16]{0:T(128)S(1)} %bitcast.10, s32[16]{0:T(128)S(1)} %bitcast.13), custom_call_target="tpu_custom_call" | custom-call | tf_op jit(solution)/shard_map/grads/pallas_call | solution.py:377
  93.4 0.0 copy-done.1
  93.4 0.0 copy-done.2
  93.4 6.6 %update.1 = (f32[2,512,512]{2,1,0:T(8,128)}, f32[2,512,512]{2,1,0:T(8,128)}, bf16[2,512,512]{2,1,0:T(8,128)(2,1)S(1)}, f32[2,2,8,128]{3,2,1,0:T(8,128)S(1)}) custom-call(s32[2]{0:T(128)S(1)} %convert_element_type.3.used_ref, bf16[4,2,512,128]{3,2,1,0:T(8,128)(2,1)S(1)} %grads.1.h_ref, f32[2,512,512]{2,1,0:T(8,128)S(1)} %bitcast.8, f32[2,512,512]{2,1,0:T(8,128)S(1)} %bitcast.9), custom_call_target="tpu_custom_call" | custom-call | tf_op jit(solution)/shard_map/update/pallas_call | solution.py:404
  100.0 52.5 %back.1 = bf16[256,512]{1,0:T(8,128)(2,1)S(1)} custom-call(bf16[2,512,512]{2,1,0:T(8,128)(2,1)S(1)} %get-tuple-element.7.p_ref, f32[2,2,8,128]{3,2,1,0:T(8,128)S(1)} %get-tuple-element.8.sum_ref, s32[16]{0:T(128)S(1)} %bitcast.11, s32[16]{0:T(128)S(1)} %bitcast.14), custom_call_target="tpu_custom_call" | custom-call | tf_op jit(solution)/shard_map/back/pallas_call | solution.py:419
  152.5 0.7 copy.10
  (1 shorter events, 0.0 us)
Async XLA Ops:
  2.1 2.2 %copy-start = (bf16[256,8192]{1,0:T(8,128)(2,1)S(1)}, bf16[256,8192]{1,0:T(8,128)(2,1)}, u32[]{:S(2)}) copy-start(bf16[256,8192]{1,0:T(8,128)(2,1)} %a_ref.1) | copy-start | bytes 12582916
  4.3 0.9 copy-start.3
  5.2 0.7 copy-start.4
  5.9 0.7 copy-start.5
  6.5 86.9 %copy-start.1 = (f32[1,1,2,512,512]{4,3,2,1,0:T(8,128)S(1)}, f32[1,1,2,512,512]{4,3,2,1,0:T(8,128)}, u32[]{:S(2)}) copy-start(f32[1,1,2,512,512]{4,3,2,1,0:T(8,128)} %param.10) | copy-start | bytes 6291460
  6.5 86.9 %copy-start.2 = (f32[1,1,2,512,512]{4,3,2,1,0:T(8,128)S(1)}, f32[1,1,2,512,512]{4,3,2,1,0:T(8,128)}, u32[]{:S(2)}) copy-start(f32[1,1,2,512,512]{4,3,2,1,0:T(8,128)} %param.11) | copy-start | bytes 6291460

commit v2 on v0

v2 whole, which is shorter than its diff:
```python
import functools

import jax
import jax.numpy as jnp
from jax import lax
from jax.experimental import pallas as pl
from jax.experimental.pallas import tpu as pltpu
from jax.sharding import PartitionSpec as P

N = 512
Q = 128
NZ, NY, NX, NT = 8, 4, 4, 8
SLOTS, NBLK, TOK = 2, 16, 256
XTOK = TOK // NX
EXTRA = 16
BETA = 0.95
MESH = pl.DeviceIdType.MESH
RIGHT, LEFT = 0, 1
bf16, f32 = jnp.bfloat16, jnp.float32


def place():
    dp, t = lax.axis_index("dp"), lax.axis_index("tensor")
    return dp, t, dp // NY, lax.rem(dp, NY)


def ring(z, step):
    return lax.rem(z + step + NZ, NZ)


def remote(src, dst, send, recv, dp, t):
    return pltpu.make_async_remote_copy(
        src_ref=src, dst_ref=dst, send_sem=send, recv_sem=recv,
        device_id=(dp, t), device_id_type=MESH,
    )


def dot(a, b, ca, cb):
    return lax.dot_general(a, b, (((ca,), (cb,)), ((), ())), preferred_element_type=f32)


def held(own_ref, slot_ref, device, slot):
    block, used = jnp.int32(0), jnp.int32(0)
    for b in range(NBLK):
        hit = (own_ref[0, b] == device) & (slot_ref[0, b] == slot)
        block = jnp.where(hit, b, block)
        used = jnp.where(hit, 1, used)
    return block, used


def chunk_of(z, k):
    far = 4 - (k + 1) // 2
    return ring(z, far if k % 2 else -far)


def moves_of(k):
    if k == 0:
        return [(RIGHT, 0, 0), (LEFT, 0, 1)]
    if k == NZ - 1:
        return []
    return [((RIGHT if k % 2 else LEFT), (k + 1) // 2, p) for p in range(2)]


def step_kernel(
    a_ref, o_ref, own_ref, slot_ref, l_ref, r_ref, out_ref, lo_ref, ro_ref,
    l_buf, r_buf, tp, got, t_snd, t_rcv, t_fin, t_all,
    a_buf, o_buf, ot_buf, snd, rcv, gath, g_all, stage, h_buf, xl_buf, pre_buf, sums,
    st_sem, out_sem, t_send, t_recv, c_send, c_recv, ta_send, ta_recv,
    o_send, o_recv, own_sem, a_send, a_recv, x_send, x_recv, f_send, f_recv,
    r_send, r_recv, g_send, g_recv, ga_send, ga_recv, y_send, y_recv, s_send, s_recv,
):
    dp, t, z, y = place()
    core, x = lax.rem(t, 2), t // 2
    twin = t + 1 - 2 * core
    xs = [lax.rem(x + i, NX) for i in range(NX)]
    xt = [2 * xi + core for xi in xs]
    ys = [lax.rem(y + j, NY) for j in range(NY)]
    ydp = [z * NY + yj for yj in ys]
    side = [ring(z, 1) * NY + y, ring(z, -1) * NY + y]
    ts = [lax.rem(t + j, NT) for j in range(NT)]
    zdp = [ring(z, j) * NY + y for j in range(NZ)]

    def behind(j):
        return ys[(NY - j) % NY]

    def columns(c, p, yj):
        return pl.ds(pl.multiple_of((2 * c + p) * N + yj * Q, Q), Q)

    state_in = [
        pltpu.make_async_copy(ref.at[s], buf.at[s], st_sem.at[i, s])
        for s in range(SLOTS)
        for i, (ref, buf) in enumerate(((l_ref, l_buf), (r_ref, r_buf)))
    ]
    for copy in state_in:
        copy.start()
    peers = (
        [(ydp[j], t) for j in range(1, NY)]
        + [(dp, ts[j]) for j in range(1, NT)]
        + [(zdp[j], t) for j in range(1, NZ)]
    )
    met = pltpu.get_barrier_semaphore()
    for peer in peers:
        pl.semaphore_signal(met, inc=1, device_id=peer, device_id_type=MESH)

    def own_copy(k, p):
        c = chunk_of(z, k)
        return pltpu.make_async_copy(
            a_ref.at[:, :, columns(c, p, y)], a_buf.at[c, p, :, 0], own_sem.at[k, p]
        )

    for k in range(NZ):
        for p in range(2):
            own_copy(k, p).start()
    o_buf[:, 0] = o_ref[...]

    row = lax.broadcasted_iota(jnp.int32, (N, N), 0)
    col = lax.broadcasted_iota(jnp.int32, (N, N), 1)
    eye = (row == col).astype(f32)

    for s in range(SLOTS):
        for copy in state_in[2 * s : 2 * s + 2]:
            copy.wait()
        both = jnp.where(row <= col, l_buf[s], r_buf[s]).astype(bf16)
        diag = jnp.sum(r_buf[s] * eye, axis=0, keepdims=True)
        diag = jnp.broadcast_to(diag, (EXTRA, N)).astype(bf16)
        for q in range(NY):
            tp[q, s, pl.ds(0, N)] = both[:, q * Q : (q + 1) * Q]
            tp[q, s, pl.ds(N, EXTRA)] = diag[:, q * Q : (q + 1) * Q]
    pl.semaphore_wait(met, len(peers))

    def t_copy(j, src):
        return remote(tp.at[ys[j]], got.at[src], t_send.at[j], t_recv.at[j], ydp[j], t)

    for j in (2, 1, 3):
        t_copy(j, y).start()
    got[y] = tp[y]

    def o_copy(j):
        return remote(o_ref, o_buf.at[:, j], o_send.at[j], o_recv.at[j], ydp[j], t)

    def a_copy(k, j):
        c = chunk_of(z, k)
        return remote(
            a_ref.at[x, :, columns(c, core, ys[j])], a_buf.at[c, core, x, j],
            a_send.at[k, j], a_recv.at[k, j], ydp[j], t,
        )

    for k in range(NZ):
        for j in (2, 1, 3):
            a_copy(k, j).start()
    for j in (2, 1, 3):
        o_copy(j).start()

    def x_copy(k, i, src):
        part = a_buf.at[chunk_of(z, k), core, src, 1:]
        return remote(part, part, x_send.at[k, i], x_recv.at[k, i], dp, xt[i])

    def f_copy(k, p):
        part = a_buf.at[chunk_of(z, k), p, :, 1:]
        return remote(part, part, f_send.at[k], f_recv.at[k], dp, twin)

    def along_x(k):
        for j in (1, 3, 2):
            a_copy(k, j).wait_recv()
        for i in (2, 1, 3):
            x_copy(k, i, x).start()

    def to_twin(k):
        for i in (1, 3, 2):
            x_copy(k, i, xs[NX - i]).wait_recv()
        f_copy(k, core).start()

    def t_chain(d, s, p):
        return remote(
            t_snd.at[d, s, p], t_rcv.at[d, s, p], c_send.at[d, s, p], c_recv.at[d, s, p], side[d], t
        )

    def place_of(c, p):
        owner = own_ref[0, 2 * c + p]
        return owner // NY, lax.rem(owner, NY), slot_ref[0, 2 * c + p]

    for j in (1, 3, 2):
        t_copy(j, behind(j)).wait_recv()
    for k in range(NZ):
        for d, s, p in moves_of(k):
            oz, oy, os = place_of(chunk_of(z, k), p)
            value = got[oy, os]
            if s > 1 or (s == 1 and p == d):
                t_chain(d, s - 1, p).wait_recv()
                value = jnp.where(oz == z, value, t_rcv[d, s - 1, p])
            t_snd[d, s, p] = value
            t_chain(d, s, p).start()
        along_x(k)
        if k >= 1:
            to_twin(k - 1)
    for p in range(2):
        oz, oy, os = place_of(z, p)
        for d in (RIGHT, LEFT):
            t_chain(d, 3, p).wait_recv()
        back = ring(z, -oz)
        from_left = (back < 4) | ((back == 4) & (p == 0))
        value = jnp.where(from_left, t_rcv[RIGHT, 3, p], t_rcv[LEFT, 3, p])
        t_fin[p] = jnp.where(oz == z, got[oy, os], value)
    to_twin(NZ - 1)

    def ta_copy(j, src):
        return remote(t_fin.at[ys[j] // 2], t_all.at[src], ta_send.at[j], ta_recv.at[j], ydp[j], t)

    def ga_copy(j, src):
        piece = gath.at[2 * z + ys[j] // 2]
        return remote(piece, g_all.at[src], ga_send.at[j], ga_recv.at[j], ydp[j], t)

    for j in (2, 1, 3):
        ta_copy(j, y).start()
    t_all[y] = t_fin[y // 2]

    def chain(d, s, p):
        return remote(
            snd.at[d, s, p], rcv.at[d, s, p], r_send.at[d, s, p], r_recv.at[d, s, p], side[d], t
        )

    for j in (1, 3, 2):
        o_copy(j).wait_recv()
    ot_buf[...] = o_buf[...].reshape(NY * TOK, N).T
    for k in range(NZ):
        c = chunk_of(z, k)
        for p in range(2):
            own_copy(k, p).wait()
        f_copy(k, 1 - core).wait_recv()
        acts = jnp.concatenate([a_buf[c, p].reshape(NY * TOK, Q) for p in range(2)], axis=1)
        part = dot(ot_buf[...], acts, 1, 0)
        part = [part[:, :Q], part[:, Q:]]
        for d, s, p in moves_of(k):
            value = part[p]
            if s > 1 or (s == 1 and p == d):
                chain(d, s - 1, p).wait_recv()
                value = value + rcv[d, s - 1, p].astype(f32)
            snd[d, s, p] = value.astype(bf16)
            chain(d, s, p).start()
    gsum = jnp.zeros((1, 1), f32)
    for p in range(2):
        for d in (RIGHT, LEFT):
            chain(d, 3, p).wait_recv()
        total = part[p] + rcv[RIGHT, 3, p].astype(f32) + rcv[LEFT, 3, p].astype(f32)
        total = total.astype(bf16)
        gath[2 * z + p] = total
        total = total.astype(f32)
        gsum = gsum + jnp.sum(total * total, axis=(0, 1), keepdims=True)

    def g_copy(d, s, p):
        piece = gath.at[2 * ring(z, -s if d == RIGHT else s) + p]
        return remote(piece, piece, g_send.at[d, s, p], g_recv.at[d, s, p], side[d], t)

    def g_wait(d, s, p):
        piece = gath.at[2 * ring(z, -s - 1 if d == RIGHT else s + 1) + p]
        remote(piece, piece, g_send.at[d, s, p], g_recv.at[d, s, p], side[d], t).wait_recv()

    def hop(s):
        for p in range(2):
            for d in (RIGHT, LEFT):
                if s < 3 or p == d:
                    if s > 0:
                        g_wait(d, s - 1, p)
                    g_copy(d, s, p).start()

    hop(0)
    for j in (2, 1, 3):
        ga_copy(j, y).start()
    g_all[y] = gath[2 * z + y // 2]

    for j in (1, 3, 2):
        ta_copy(j, behind(j)).wait_recv()
    both = jnp.concatenate([t_all[q, pl.ds(0, N)] for q in range(NY)], axis=1)
    diag = jnp.concatenate([t_all[q, pl.ds(N, EXTRA)] for q in range(NY)], axis=1)[0:1]
    flip = both.T.astype(f32)
    both = both.astype(f32)
    l_old = jnp.where(row <= col, both, flip)
    r_old = jnp.where(row > col, both, flip)
    r_old = jnp.where(row == col, diag.astype(f32), r_old)
    for j in (1, 3, 2):
        ga_copy(j, behind(j)).wait_recv()
    hop(1)
    h = jnp.concatenate([g_all[q] for q in range(NY)], axis=1)
    xr = root(BETA * r_old + dot(h, h, 1, 1), eye)
    part = dot(xr, h, 1, 0).astype(bf16)
    xl_buf[...] = root(BETA * l_old + dot(h, h, 0, 0), eye)
    half = xl_buf[pl.ds(pl.multiple_of(lax.rem(y, 2) * TOK, TOK), TOK)]
    pre = dot(half, part, 1, 1).astype(bf16)
    pre_buf[...] = pre
    pf = pre.astype(f32)
    psum = jnp.sum(pf * pf, axis=(0, 1), keepdims=True)

    stages = [
        (NT, lambda j: (dp, ts[j])),
        (NY, lambda j: (ydp[j], t)),
        (NZ, lambda j: (zdp[j], t)),
    ]

    def s_copy(i, j):
        return remote(
            sums.at[i, 0], sums.at[i, j], s_send.at[i, j], s_recv.at[i, j], *stages[i][1](j)
        )

    def sum_start(i, value):
        sums[i, 0] = value
        for j in range(1, stages[i][0]):
            s_copy(i, j).start()

    def sum_end(i):
        for j in range(1, stages[i][0]):
            s_copy(i, j).wait_recv()
        return functools.reduce(jnp.add, [sums[i, j] for j in range(stages[i][0])])

    sum_start(0, jnp.stack([jnp.broadcast_to(v, (8, 128)) for v in (gsum, psum)]))
    hop(2)
    sum_start(1, sum_end(0))
    sum_start(2, sum_end(1))
    hop(3)
    total = sum_end(2)
    ratio = jnp.sqrt(total[0] / total[1])[0:1, 0:1]
    out_ref[...] = (pre_buf[...].astype(f32) * ratio).astype(bf16)

    def y_copy(j, src):
        return remote(stage.at[j], h_buf.at[src], y_send.at[j], y_recv.at[j], ydp[j], t)

    picks = [[held(own_ref, slot_ref, ydp[j], s) for s in range(SLOTS)] for j in range(NY)]
    for d in (RIGHT, LEFT):
        g_wait(d, 2, 1 - d)
        g_wait(d, 3, d)
    for j in (2, 1, 3, 0):
        for s in range(SLOTS):
            if j:
                stage[j, s] = gath[picks[j][s][0]]
            else:
                h_buf[y, s] = gath[picks[j][s][0]]
        if j:
            y_copy(j, y).start()
    for j in (1, 3, 2):
        y_copy(j, behind(j)).wait_recv()
    state_out = []
    for s in range(SLOTS):
        used = picks[0][s][1] != 0
        h = jnp.concatenate([h_buf[q, s] for q in range(NY)], axis=1)
        for i, (ref, buf, axis) in enumerate(((lo_ref, l_buf, 0), (ro_ref, r_buf, 1))):
            old = buf[s]
            buf[s] = jnp.where(used, BETA * old + dot(h, h, axis, axis), old)
            state_out.append(pltpu.make_async_copy(buf.at[s], ref.at[s], out_sem.at[i, s]))
            state_out[-1].start()

    for j in (1, 2, 3):
        t_copy(j, y).wait_send()
        o_copy(j).wait_send()
        ta_copy(j, y).wait_send()
        ga_copy(j, y).wait_send()
        y_copy(j, y).wait_send()
    for k in range(NZ):
        f_copy(k, core).wait_send()
        for j in (1, 2, 3):
            a_copy(k, j).wait_send()
            x_copy(k, j, x).wait_send()
        for d, s, p in moves_of(k):
            t_chain(d, s, p).wait_send()
            chain(d, s, p).wait_send()
            if s < 3 or p == d:
                g_copy(d, s, p).wait_send()
    for d in (RIGHT, LEFT):
        g_copy(d, 0, 1 - d).wait_send()
    for i in range(3):
        for j in range(1, stages[i][0]):
            s_copy(i, j).wait_send()
    for copy in state_out:
        copy.wait()


def root(mat, eye):
    norm = jnp.sqrt(jnp.sum(mat * mat, axis=(0, 1), keepdims=True))
    scale = 2.5 / norm
    m = mat * scale
    mb = m.astype(bf16)
    square = dot(mb, mb, 1, 0)
    s2 = (1.5625 * eye - 0.625 * m + 0.0625 * square).astype(bf16)
    sm = (1.25 * m - 0.25 * square).astype(bf16)
    s4 = dot(s2, s2, 1, 0).astype(bf16)
    x = 1.5625 * eye - 0.3125 * m - 0.25 * dot(s4, sm, 1, 0)
    return (x * jnp.sqrt(jnp.sqrt(scale))).astype(bf16)


VMEM = pl.BlockSpec(memory_space=pltpu.VMEM)
SMEM = pl.BlockSpec(memory_space=pltpu.SMEM)
HBM = pl.BlockSpec(memory_space=pltpu.MemorySpace.HBM)
DMA = pltpu.SemaphoreType.DMA


def shards(activations, out_grads, owner, slot, left_state, right_state):
    direction, left_out, right_out = pl.pallas_call(
        step_kernel,
        out_shape=[
            jax.ShapeDtypeStruct((TOK, N), bf16),
            jax.ShapeDtypeStruct((SLOTS, N, N), f32),
            jax.ShapeDtypeStruct((SLOTS, N, N), f32),
        ],
        in_specs=[HBM, VMEM, SMEM, SMEM, HBM, HBM],
        out_specs=[VMEM, HBM, HBM],
        scratch_shapes=[
            pltpu.VMEM((SLOTS, N, N), f32),
            pltpu.VMEM((SLOTS, N, N), f32),
            pltpu.VMEM((NY, SLOTS, N + EXTRA, Q), bf16),
            pltpu.VMEM((NY, SLOTS, N + EXTRA, Q), bf16),
            pltpu.VMEM((2, 4, 2, N + EXTRA, Q), bf16),
            pltpu.VMEM((2, 4, 2, N + EXTRA, Q), bf16),
            pltpu.VMEM((2, N + EXTRA, Q), bf16),
            pltpu.VMEM((NY, N + EXTRA, Q), bf16),
            pltpu.VMEM((NZ, 2, NX, NY, XTOK, Q), bf16),
            pltpu.VMEM((NX, NY, XTOK, N), bf16),
            pltpu.VMEM((N, NY * TOK), bf16),
            pltpu.VMEM((2, 4, 2, N, Q), bf16),
            pltpu.VMEM((2, 4, 2, N, Q), bf16),
            pltpu.VMEM((NBLK, N, Q), bf16),
            pltpu.VMEM((NY, N, Q), bf16),
            pltpu.VMEM((NY, SLOTS, N, Q), bf16),
            pltpu.VMEM((NY, SLOTS, N, Q), bf16),
            pltpu.VMEM((N, N), bf16),
            pltpu.VMEM((TOK, N), bf16),
            pltpu.VMEM((3, NT, 2, 8, 128), f32),
            DMA((2, SLOTS)), DMA((2, SLOTS)),
            DMA((NY,)), DMA((NY,)),
            DMA((2, 4, 2)), DMA((2, 4, 2)),
            DMA((NY,)), DMA((NY,)),
            DMA((NY,)), DMA((NY,)),
            DMA((NZ, 2)),
            DMA((NZ, NY)), DMA((NZ, NY)),
            DMA((NZ, NX)), DMA((NZ, NX)),
            DMA((NZ,)), DMA((NZ,)),
            DMA((2, 4, 2)), DMA((2, 4, 2)),
            DMA((2, 4, 2)), DMA((2, 4, 2)),
            DMA((NY,)), DMA((NY,)),
            DMA((NY,)), DMA((NY,)),
            DMA((3, NT)), DMA((3, NT)),
        ],
        compiler_params=pltpu.CompilerParams(
            collective_id=0, has_side_effects=True, vmem_limit_bytes=56 * 2**20
        ),
        name="step",
    )(
        activations.reshape(NX, XTOK, -1), out_grads.reshape(NX, XTOK, N), owner, slot,
        left_state[0, 0], right_state[0, 0],
    )
    return direction, left_out[None, None], right_out[None, None]


def solution(mesh):
    return jax.shard_map(
        shards,
        mesh=mesh,
        in_specs=(
            P("dp", None),
            P("dp", "tensor"),
            P("tensor", None),
            P("tensor", None),
            P("tensor", "dp", None, None, None),
            P("tensor", "dp", None, None, None),
        ),
        out_specs=(
            P("dp", "tensor"),
            P("tensor", "dp", None, None, None),
            P("tensor", "dp", None, None, None),
        ),
        check_vma=False,
    )
```

time: 806 us -> 132 us (0.16); the launches traced: 796 us -> 132 us
  waiting for transfers between devices: 585 us -> 0 us
  Pallas kernels: 0 us -> 125 us
  blocking collectives: 80 us -> 0 us
  matrix products: 59.8 us -> 0 us
  other arithmetic: 30.8 us -> 0 us
  between operations: 15.8 us -> 0.64 us
  starting transfers between devices: 14.3 us -> 0 us
    all_to_all x2 -> x0, waiting for transfers between devices: 358 us -> none  [the longest x1 181 us: send_back(): lax.all_to_all(outgoing, 'dp', split_axis=0, concat_axis=0, tiled=True)]
    reduce_scatter x1 -> x0, waiting for transfers between devices: 227 us -> none  [shards(): lax.psum_scatter(jnp.einsum('tr,tc->rc', activations, out_grads, preferre...]
    pallas_call x0 -> x1, Pallas kernels: none -> 125 us  [shards(): pl.pallas_call(step_kernel, out_shape=[jax.ShapeDtypeStruct((TOK, N), bf1...]
    psum x1 -> x0, blocking collectives: 80 us -> none  [shards(): grad_total, pre_total = lax.psum((grad_sq, pre_sq), ('dp', 'tensor'))]
    dot_general x10 -> x0, matrix products: 59.8 us -> none  [the longest x7 48.6 us: matrix_multiply(): return jnp.matmul(left, right, precision=lax.Precision.HIGHEST)]
    all_to_all x2 -> x0, starting transfers between devices: 14.3 us -> none  [the longest x1 7.23 us: shards(): lax.all_to_all(outgoing, 'dp', split_axis=0, concat_axis=0, tiled=True)]
    select_n x6 -> x0, other arithmetic: 12.6 us -> none  [the longest x1 7.57 us: send_back(): jnp.where((own == device_self)[:, :, None, None], pick, jnp.zeros((), jnp...]
    gather x2 -> x0, local copies, waits for them, and re-layouts: 8.86 us -> none  [the longest x1 4.86 us: send_back(): pick = jnp.take(out_pieces, (held * spans + span).reshape(-1), axis=0)]
  transfers between devices with their start and end apart: 3 -> 0, of which waited for: 3 -> 0; matrix products, arithmetic and copies ran while one was open for 1% -> 0% of each run, Pallas kernels for 0% -> 0%
where the time goes in v2:
time: 132 us
  Pallas kernels  125 us (95%)
  local copies, waits for them, and re-layouts  6.22 us (5%)
    pallas_call x1, Pallas kernels, shards(): pl.pallas_call(step_kernel, out_shape=[jax.ShapeDtypeStruct((TOK, N), bf1...  125 us
    unnamed x5, local copies, waits for them, and re-layouts  6.22 us

profile of v2, /device:TPU:1, one launch (start us, length us, event | category | flops | bytes accessed | tf_op | source)
XLA Modules:
  0.0 132.0 jit_solution(5144812870553087664)
XLA Ops:
  0.6 125.2 %step.1 = (bf16[256,512]{1,0:T(8,128)(2,1)}, f32[2,512,512]{2,1,0:T(8,128)}, f32[2,512,512]{2,1,0:T(8,128)}) custom-call(bf16[4,64,8192]{2,1,0:T(8,128)(2,1)} %bitcast.6, bf16[4,64,512]{2,1,0:T(8,128)(2,1)} %bitcast.11, s32[1,16]{1,0:T(1,128)} %own_ref.1, s32[1,16]{1,0:T(1,128)} %slot_ref.1, f32[2,512,512]{2,1,0:T(8,128)} %bitcast.7, f32[2,512,512]{2,1,0:T(8,128)} %bitcast.8), custom_call_target="tpu_custom_call" | custom-call | tf_op jit(solution)/shard_map/step/pallas_call | solution.py:395
  125.8 1.7 %copy.12 = bf16[256,512]{1,0:T(8,128)(2,1)} copy(bf16[256,512]{1,0:T(8,128)(2,1)} %get-tuple-element.12) | data formatting | bytes 524288
  127.5 0.0 copy-start
  127.5 3.2 %copy.13 = f32[1,1,2,512,512]{4,3,2,1,0:T(8,128)} copy(f32[1,1,2,512,512]{4,3,2,1,0:T(8,128)} %bitcast.10) | data formatting | bytes 4194304
  130.7 0.0 copy-done
  130.7 1.3 copy.14
Async XLA Ops:
  127.5 3.2 %copy-start = (f32[2,512,512]{2,1,0:T(8,128)S(1)}, f32[2,512,512]{2,1,0:T(8,128)}, u32[]{:S(2)}) copy-start(f32[2,512,512]{2,1,0:T(8,128)} %get-tuple-element.8) | copy-start | bytes 6291460

commit v3 on v2

v3 whole, which is shorter than its diff:
```python
import functools

import jax
import jax.numpy as jnp
from jax import lax
from jax.experimental import pallas as pl
from jax.experimental.pallas import tpu as pltpu
from jax.sharding import PartitionSpec as P

N = 512
HALF = 256
Q = 128
NZ, NY, NT = 8, 4, 8
SLOTS, NBLK, TOK = 2, 16, 256
EXTRA = 16
BETA = 0.95
MESH = pl.DeviceIdType.MESH
RIGHT, LEFT = 0, 1
bf16, f32 = jnp.bfloat16, jnp.float32


def place():
    dp, t = lax.axis_index("dp"), lax.axis_index("tensor")
    return dp, t, dp // NY, lax.rem(dp, NY)


def ring(z, step):
    return lax.rem(z + step + NZ, NZ)


def remote(src, dst, send, recv, dp, t):
    return pltpu.make_async_remote_copy(
        src_ref=src, dst_ref=dst, send_sem=send, recv_sem=recv,
        device_id=(dp, t), device_id_type=MESH,
    )


def dot(a, b, ca, cb):
    return lax.dot_general(a, b, (((ca,), (cb,)), ((), ())), preferred_element_type=f32)


def held(own_ref, slot_ref, device, slot):
    block, used = jnp.int32(0), jnp.int32(0)
    for b in range(NBLK):
        hit = (own_ref[0, b] == device) & (slot_ref[0, b] == slot)
        block = jnp.where(hit, b, block)
        used = jnp.where(hit, 1, used)
    return block, used


def chunk_of(z, k):
    far = 4 - (k + 1) // 2
    return ring(z, far if k % 2 else -far)


def moves_of(k):
    if k == 0:
        return [(RIGHT, 0, 0), (LEFT, 0, 1)]
    if k == NZ - 1:
        return []
    return [((RIGHT if k % 2 else LEFT), (k + 1) // 2, p) for p in range(2)]


def step_kernel(
    a_ref, o_ref, own_ref, slot_ref, l_ref, r_ref, out_ref, h_ref,
    l_buf, r_buf, tp, got, t_snd, t_rcv, t_fin, t_all,
    a_buf, ot_buf, snd, rcv, gath_0, gath_1, g_all, stage, xl_buf, pre_buf, sums,
    st_sem, t_send, t_recv, c_send, c_recv, ta_send, ta_recv,
    o_send, o_recv, own_sem, a_send, a_recv, f_send, f_recv,
    r_send, r_recv, g_send, g_recv, ga_send, ga_recv, y_send, y_recv, s_send, s_recv,
):
    dp, t, z, y = place()
    core = lax.rem(t, 2)
    gath = (gath_0, gath_1)
    twin = t + 1 - 2 * core
    ys = [lax.rem(y + j, NY) for j in range(NY)]
    ydp = [z * NY + yj for yj in ys]
    side = [ring(z, 1) * NY + y, ring(z, -1) * NY + y]
    ts = [lax.rem(t + j, NT) for j in range(NT)]
    zdp = [ring(z, j) * NY + y for j in range(NZ)]

    def behind(j):
        return ys[(NY - j) % NY]

    def columns(c, p, yj):
        return pl.ds(pl.multiple_of((2 * c + p) * N + yj * Q, Q), Q)

    state_in = [
        pltpu.make_async_copy(ref.at[s], buf.at[s], st_sem.at[i, s])
        for s in range(SLOTS)
        for i, (ref, buf) in enumerate(((l_ref, l_buf), (r_ref, r_buf)))
    ]
    for copy in state_in:
        copy.start()
    peers = (
        [(ydp[j], t) for j in range(1, NY)]
        + [(dp, ts[j]) for j in range(1, NT)]
        + [(zdp[j], t) for j in range(1, NZ)]
    )
    met = pltpu.get_barrier_semaphore()
    for peer in peers:
        pl.semaphore_signal(met, inc=1, device_id=peer, device_id_type=MESH)

    def own_copy(k, p):
        c = chunk_of(z, k)
        return pltpu.make_async_copy(
            a_ref.at[:, columns(c, p, y)], a_buf.at[c, p, 0], own_sem.at[k, p]
        )

    for k in range(NZ):
        for p in range(2):
            own_copy(k, p).start()
    ot_buf[0] = o_ref[...].T

    row = lax.broadcasted_iota(jnp.int32, (N, N), 0)
    col = lax.broadcasted_iota(jnp.int32, (N, N), 1)
    def t_copy(j, s, src):
        return remote(
            tp.at[ys[j], s], got.at[src, s], t_send.at[j, s], t_recv.at[j, s], ydp[j], t
        )

    for s in range(SLOTS):
        for copy in state_in[2 * s : 2 * s + 2]:
            copy.wait()
        both = jnp.where(row <= col, l_buf[s], r_buf[s]).astype(bf16)
        diag = jnp.sum(jnp.where(row == col, r_buf[s], 0.0), axis=0, keepdims=True)
        diag = jnp.broadcast_to(diag, (EXTRA, N)).astype(bf16)
        for q in range(NY):
            tp[q, s, pl.ds(0, N)] = both[:, q * Q : (q + 1) * Q]
            tp[q, s, pl.ds(N, EXTRA)] = diag[:, q * Q : (q + 1) * Q]
        if s == 0:
            pl.semaphore_wait(met, len(peers))
        for j in (2, 1, 3):
            t_copy(j, s, y).start()

    def o_copy(j):
        return remote(ot_buf.at[0], ot_buf.at[j], o_send.at[j], o_recv.at[j], ydp[j], t)

    def a_copy(k, j):
        c = chunk_of(z, k)
        return remote(
            a_ref.at[:, columns(c, core, ys[j])], a_buf.at[c, core, j],
            a_send.at[k, j], a_recv.at[k, j], ydp[j], t,
        )

    def f_copy(k, p):
        part = a_buf.at[chunk_of(z, k), p, 1:]
        return remote(part, part, f_send.at[k], f_recv.at[k], dp, twin)

    def to_twin(k):
        for j in (1, 3, 2):
            a_copy(k, j).wait_recv()
        f_copy(k, core).start()

    for j in (2, 1, 3):
        o_copy(j).start()
    for k in range(NZ):
        for j in (2, 1, 3):
            a_copy(k, j).start()
    got[y] = tp[y]

    def t_chain(d, s, p):
        return remote(
            t_snd.at[d, s, p], t_rcv.at[d, s, p], c_send.at[d, s, p], c_recv.at[d, s, p], side[d], t
        )

    def place_of(c, p):
        owner = own_ref[0, 2 * c + p]
        return owner // NY, lax.rem(owner, NY), slot_ref[0, 2 * c + p]

    for s in range(SLOTS):
        for j in (1, 3, 2):
            t_copy(j, s, behind(j)).wait_recv()
    for k in range(NZ):
        for d, s, p in moves_of(k):
            oz, oy, os = place_of(chunk_of(z, k), p)
            value = got[oy, os]
            if s > 1 or (s == 1 and p == d):
                t_chain(d, s - 1, p).wait_recv()
                value = jnp.where(oz == z, value, t_rcv[d, s - 1, p])
            t_snd[d, s, p] = value
            t_chain(d, s, p).start()
    for p in range(2):
        oz, oy, os = place_of(z, p)
        for d in (RIGHT, LEFT):
            t_chain(d, 3, p).wait_recv()
        back = ring(z, -oz)
        from_left = (back < 4) | ((back == 4) & (p == 0))
        value = jnp.where(from_left, t_rcv[RIGHT, 3, p], t_rcv[LEFT, 3, p])
        t_fin[p] = jnp.where(oz == z, got[oy, os], value)

    def ta_copy(j, src):
        return remote(t_fin.at[ys[j] // 2], t_all.at[src], ta_send.at[j], ta_recv.at[j], ydp[j], t)

    def ga_copy(j, src, i):
        piece = gath[i].at[2 * z + ys[j] // 2]
        return remote(piece, g_all.at[src, i], ga_send.at[j, i], ga_recv.at[j, i], ydp[j], t)

    for j in (2, 1, 3):
        ta_copy(j, y).start()
    t_all[y] = t_fin[y // 2]

    def chain(d, s, p):
        return remote(
            snd.at[d, s, p], rcv.at[d, s, p], r_send.at[d, s, p], r_recv.at[d, s, p], side[d], t
        )

    for j in (1, 3, 2):
        o_copy(j).wait_recv()
    outs = jnp.concatenate([ot_buf[j] for j in range(NY)], axis=1)
    to_twin(0)
    for k in range(NZ):
        c = chunk_of(z, k)
        if k + 1 < NZ:
            to_twin(k + 1)
        for p in range(2):
            own_copy(k, p).wait()
        f_copy(k, 1 - core).wait_recv()
        acts = jnp.concatenate([a_buf[c, p].reshape(NY * TOK, Q) for p in range(2)], axis=1)
        part = dot(outs, acts, 1, 0)
        part = [part[:, :Q], part[:, Q:]]
        for d, s, p in moves_of(k):
            value = part[p]
            if s > 1 or (s == 1 and p == d):
                chain(d, s - 1, p).wait_recv()
                value = value + rcv[d, s - 1, p].astype(f32)
            snd[d, s, p] = value.astype(bf16)
            chain(d, s, p).start()
    gsum = jnp.zeros((1, 1), f32)
    for p in range(2):
        for d in (RIGHT, LEFT):
            chain(d, 3, p).wait_recv()
        total = part[p] + rcv[RIGHT, 3, p].astype(f32) + rcv[LEFT, 3, p].astype(f32)
        total = total.astype(bf16)
        for i in range(2):
            gath[i][2 * z + p] = total[i * HALF : (i + 1) * HALF]
        total = total.astype(f32)
        gsum = gsum + jnp.sum(total * total, axis=(0, 1), keepdims=True)

    def g_copy(d, s, p, i):
        piece = gath[i].at[2 * ring(z, -s if d == RIGHT else s) + p]
        return remote(piece, piece, g_send.at[d, s, p, i], g_recv.at[d, s, p, i], side[d], t)

    def g_wait(d, s, p, i):
        piece = gath[i].at[2 * ring(z, -s - 1 if d == RIGHT else s + 1) + p]
        remote(
            piece, piece, g_send.at[d, s, p, i], g_recv.at[d, s, p, i], side[d], t
        ).wait_recv()

    def hop(s, i):
        for p in range(2):
            for d in (RIGHT, LEFT):
                if s < 3 or p == d:
                    if s > 0:
                        g_wait(d, s - 1, p, i)
                    g_copy(d, s, p, i).start()

    def y_copy(j, src, i):
        return remote(
            stage.at[i, j], h_ref.at[i, src], y_send.at[i, j], y_recv.at[i, j], ydp[j], t
        )

    picks = [[held(own_ref, slot_ref, ydp[j], s)[0] for s in range(SLOTS)] for j in range(NY)]

    def to_owners(i):
        for d in (RIGHT, LEFT):
            g_wait(d, 2, 1 - d, i)
            g_wait(d, 3, d, i)
        for j in (2, 1, 3, 0):
            for s in range(SLOTS):
                if j:
                    stage[i, j, s] = gath[i][picks[j][s]]
                else:
                    h_ref[i, y, s] = gath[i][picks[j][s]]
            if j:
                y_copy(j, y, i).start()

    hop(0, 0)
    hop(0, 1)
    for j in (2, 1, 3):
        for i in range(2):
            ga_copy(j, y, i).start()
    for i in range(2):
        g_all[y, i] = gath[i][2 * z + y // 2]

    eye = (row == col).astype(f32)
    for j in (1, 3, 2):
        ta_copy(j, behind(j)).wait_recv()
    both = jnp.concatenate([t_all[q, pl.ds(0, N)] for q in range(NY)], axis=1)
    diag = jnp.concatenate([t_all[q, pl.ds(N, EXTRA)] for q in range(NY)], axis=1)[0:1]
    flip = both.T.astype(f32)
    both = both.astype(f32)
    l_old = jnp.where(row <= col, both, flip)
    r_old = jnp.where(row > col, both, flip)
    r_old = jnp.where(row == col, diag.astype(f32), r_old)
    hop(1, 0)
    for j in (1, 3, 2):
        for i in range(2):
            ga_copy(j, behind(j), i).wait_recv()
    hop(2, 0)
    hop(1, 1)
    h = jnp.concatenate([g_all[q].reshape(N, Q) for q in range(NY)], axis=1)
    xr = root(BETA * r_old + dot(h, h, 1, 1), eye)
    part = dot(xr, h, 1, 0).astype(bf16)
    xl_buf[...] = root(BETA * l_old + dot(h, h, 0, 0), eye)
    half = xl_buf[pl.ds(pl.multiple_of(lax.rem(y, 2) * TOK, TOK), TOK)]
    pre = dot(half, part, 1, 1).astype(bf16)
    pre_buf[...] = pre
    pf = pre.astype(f32)
    psum = jnp.sum(pf * pf, axis=(0, 1), keepdims=True)

    stages = [
        (NT, lambda j: (dp, ts[j])),
        (NY, lambda j: (ydp[j], t)),
        (NZ, lambda j: (zdp[j], t)),
    ]

    def s_copy(i, j):
        return remote(
            sums.at[i, 0], sums.at[i, j], s_send.at[i, j], s_recv.at[i, j], *stages[i][1](j)
        )

    def sum_start(i, value):
        sums[i, 0] = value
        for j in range(1, stages[i][0]):
            s_copy(i, j).start()

    def sum_end(i):
        for j in range(1, stages[i][0]):
            s_copy(i, j).wait_recv()
        return functools.reduce(jnp.add, [sums[i, j] for j in range(stages[i][0])])

    sum_start(0, jnp.stack([jnp.broadcast_to(v, (8, 128)) for v in (gsum, psum)]))
    hop(3, 0)
    hop(2, 1)
    sum_start(1, sum_end(0))
    hop(3, 1)
    sum_start(2, sum_end(1))
    to_owners(0)
    to_owners(1)
    total = sum_end(2)
    ratio = jnp.sqrt(total[0] / total[1])[0:1, 0:1]
    out_ref[...] = (pre_buf[...].astype(f32) * ratio).astype(bf16)

    for i in range(2):
        for j in (1, 3, 2):
            y_copy(j, behind(j), i).wait_recv()

    for j in (1, 2, 3):
        for s in range(SLOTS):
            t_copy(j, s, y).wait_send()
        o_copy(j).wait_send()
        ta_copy(j, y).wait_send()
        for i in range(2):
            ga_copy(j, y, i).wait_send()
        for i in range(2):
            y_copy(j, y, i).wait_send()
    for k in range(NZ):
        f_copy(k, core).wait_send()
        for j in (1, 2, 3):
            a_copy(k, j).wait_send()
        for d, s, p in moves_of(k):
            t_chain(d, s, p).wait_send()
            chain(d, s, p).wait_send()
            if s < 3 or p == d:
                for i in range(2):
                    g_copy(d, s, p, i).wait_send()
    for d in (RIGHT, LEFT):
        for i in range(2):
            g_copy(d, 0, 1 - d, i).wait_send()
    for i in range(3):
        for j in range(1, stages[i][0]):
            s_copy(i, j).wait_send()


def update_kernel(own_ref, slot_ref, h_ref, l_ref, r_ref, lo_ref, ro_ref):
    _, used = held(own_ref, slot_ref, lax.axis_index("dp"), pl.program_id(0))

    @pl.when(used == 0)
    def _():
        lo_ref[...] = l_ref[...]
        ro_ref[...] = r_ref[...]

    @pl.when(used != 0)
    def _():
        h = jnp.concatenate([h_ref[:, q, 0].reshape(N, Q) for q in range(NY)], axis=1)
        lo_ref[0] = BETA * l_ref[0] + dot(h, h, 0, 0)
        ro_ref[0] = BETA * r_ref[0] + dot(h, h, 1, 1)


def root(mat, eye):
    norm = jnp.sqrt(jnp.sum(mat * mat, axis=(0, 1), keepdims=True))
    scale = 2.5 / norm
    m = mat * scale
    mb = m.astype(bf16)
    square = dot(mb, mb, 1, 0)
    s2 = (1.5625 * eye - 0.625 * m + 0.0625 * square).astype(bf16)
    sm = (1.25 * m - 0.25 * square).astype(bf16)
    s4 = dot(s2, s2, 1, 0).astype(bf16)
    x = 1.5625 * eye - 0.3125 * m - 0.25 * dot(s4, sm, 1, 0)
    return (x * jnp.sqrt(jnp.sqrt(scale))).astype(bf16)


VMEM = pl.BlockSpec(memory_space=pltpu.VMEM)
SMEM = pl.BlockSpec(memory_space=pltpu.SMEM)
HBM = pl.BlockSpec(memory_space=pltpu.MemorySpace.HBM)
DMA = pltpu.SemaphoreType.DMA


def shards(activations, out_grads, owner, slot, left_state, right_state):
    direction, h = pl.pallas_call(
        step_kernel,
        out_shape=[
            jax.ShapeDtypeStruct((TOK, N), bf16),
            jax.ShapeDtypeStruct((2, NY, SLOTS, HALF, Q), bf16),
        ],
        in_specs=[HBM, VMEM, SMEM, SMEM, HBM, HBM],
        out_specs=[VMEM, VMEM],
        scratch_shapes=[
            pltpu.VMEM((SLOTS, N, N), f32),
            pltpu.VMEM((SLOTS, N, N), f32),
            pltpu.VMEM((NY, SLOTS, N + EXTRA, Q), bf16),
            pltpu.VMEM((NY, SLOTS, N + EXTRA, Q), bf16),
            pltpu.VMEM((2, 4, 2, N + EXTRA, Q), bf16),
            pltpu.VMEM((2, 4, 2, N + EXTRA, Q), bf16),
            pltpu.VMEM((2, N + EXTRA, Q), bf16),
            pltpu.VMEM((NY, N + EXTRA, Q), bf16),
            pltpu.VMEM((NZ, 2, NY, TOK, Q), bf16),
            pltpu.VMEM((NY, N, TOK), bf16),
            pltpu.VMEM((2, 4, 2, N, Q), bf16),
            pltpu.VMEM((2, 4, 2, N, Q), bf16),
            pltpu.VMEM((NBLK, HALF, Q), bf16),
            pltpu.VMEM((NBLK, HALF, Q), bf16),
            pltpu.VMEM((NY, 2, HALF, Q), bf16),
            pltpu.VMEM((2, NY, SLOTS, HALF, Q), bf16),
            pltpu.VMEM((N, N), bf16),
            pltpu.VMEM((TOK, N), bf16),
            pltpu.VMEM((3, NT, 2, 8, 128), f32),
            DMA((2, SLOTS)),
            DMA((NY, SLOTS)), DMA((NY, SLOTS)),
            DMA((2, 4, 2)), DMA((2, 4, 2)),
            DMA((NY,)), DMA((NY,)),
            DMA((NY,)), DMA((NY,)),
            DMA((NZ, 2)),
            DMA((NZ, NY)), DMA((NZ, NY)),
            DMA((NZ,)), DMA((NZ,)),
            DMA((2, 4, 2)), DMA((2, 4, 2)),
            DMA((2, 4, 2, 2)), DMA((2, 4, 2, 2)),
            DMA((NY, 2)), DMA((NY, 2)),
            DMA((2, NY)), DMA((2, NY)),
            DMA((3, NT)), DMA((3, NT)),
        ],
        compiler_params=pltpu.CompilerParams(
            collective_id=0, has_side_effects=True, vmem_limit_bytes=56 * 2**20
        ),
        name="step",
    )(
        activations, out_grads, owner, slot,
        left_state[0, 0], right_state[0, 0],
    )
    state = pl.BlockSpec((1, N, N), lambda s: (s, 0, 0))
    left_out, right_out = pl.pallas_call(
        update_kernel,
        grid=(SLOTS,),
        out_shape=[jax.ShapeDtypeStruct((SLOTS, N, N), f32)] * 2,
        in_specs=[
            SMEM, SMEM, pl.BlockSpec((2, NY, 1, HALF, Q), lambda s: (0, 0, s, 0, 0)), state, state,
        ],
        out_specs=[state, state],
        compiler_params=pltpu.CompilerParams(vmem_limit_bytes=24 * 2**20),
        name="update",
    )(owner, slot, h, left_state[0, 0], right_state[0, 0])
    return direction, left_out[None, None], right_out[None, None]


def solution(mesh):
    return jax.shard_map(
        shards,
        mesh=mesh,
        in_specs=(
            P("dp", None),
            P("dp", "tensor"),
            P("tensor", None),
            P("tensor", None),
            P("tensor", "dp", None, None, None),
            P("tensor", "dp", None, None, None),
        ),
        out_specs=(
            P("dp", "tensor"),
            P("tensor", "dp", None, None, None),
            P("tensor", "dp", None, None, None),
        ),
        check_vma=False,
    )
```

time: 132 us -> 127 us (0.962)
  local copies, waits for them, and re-layouts: 6.22 us -> 1.94 us
    unnamed x5 -> x13, local copies, waits for them, and re-layouts: 6.22 us -> 1.94 us
    pallas_call x1, Pallas kernels: 125 us -> 121 us  [shards(): pl.pallas_call(step_kernel, out_shape=[jax.ShapeDtypeStruct((TOK, N), bf1...]
    pallas_call x0 -> x1, Pallas kernels: none -> 2.78 us  [shards(): pl.pallas_call(update_kernel, grid=(SLOTS,), out_shape=[jax.ShapeDtypeStr...]
where the time goes in v3:
time: 127 us
  Pallas kernels  124 us (98%)
  local copies, waits for them, and re-layouts  1.94 us (2%)
    pallas_call x1, Pallas kernels, shards(): pl.pallas_call(step_kernel, out_shape=[jax.ShapeDtypeStruct((TOK, N), bf1...  121 us
    pallas_call x1, Pallas kernels, shards(): pl.pallas_call(update_kernel, grid=(SLOTS,), out_shape=[jax.ShapeDtypeStr...  2.78 us

profile of v3, /device:TPU:1, one launch (start us, length us, event | category | flops | bytes accessed | tf_op | source)
XLA Modules:
  0.0 126.7 jit_solution(17021074492091611935)
XLA Ops:
  0.6 0.0 copy-start
  0.6 0.0 copy-start.1
  0.7 0.0 copy-start.3
  0.7 0.0 copy-start.4
  0.7 121.3 %step.1 = (bf16[256,512]{1,0:T(8,128)(2,1)}, bf16[2,4,2,256,128]{4,3,2,1,0:T(8,128)(2,1)}) custom-call(bf16[256,8192]{1,0:T(8,128)(2,1)} %a_ref.1, bf16[256,512]{1,0:T(8,128)(2,1)} %o_ref.1, s32[1,16]{1,0:T(1,128)} %own_ref.3, s32[1,16]{1,0:T(1,128)} %slot_ref.3, f32[2,512,512]{2,1,0:T(8,128)} %bitcast.4, f32[2,512,512]{2,1,0:T(8,128)} %bitcast.6), custom_call_target="tpu_custom_call" | custom-call | tf_op jit(solution)/shard_map/step/pallas_call | solution.py:411
  122.0 0.0 copy-done
  122.0 0.0 copy-done.1
  122.0 0.0 copy-done.3
  122.0 0.0 copy-done.4
  122.0 0.0 copy-start.2
  122.0 1.2 copy-done.2
  123.2 0.0 copy-start.5
  123.2 2.8 %update.1 = (f32[2,512,512]{2,1,0:T(8,128)}, f32[2,512,512]{2,1,0:T(8,128)}) custom-call(s32[1,16]{1,0:T(1,128)S(1)} %copy-done.3, s32[1,16]{1,0:T(1,128)S(1)} %copy-done.4, bf16[2,4,2,256,128]{4,3,2,1,0:T(8,128)(2,1)S(1)} %copy-done.2, f32[2,512,512]{2,1,0:T(8,128)S(1)} %bitcast.5, f32[2,512,512]{2,1,0:T(8,128)S(1)} %bitcast.7), custom_call_target="tpu_custom_call" | custom-call | tf_op jit(solution)/shard_map/update/pallas_call | solution.py:462
  126.0 0.0 copy-done.5
  126.0 0.7 copy.10
Async XLA Ops:
  0.6 121.3 %copy-start = (f32[1,1,2,512,512]{4,3,2,1,0:T(8,128)S(1)}, f32[1,1,2,512,512]{4,3,2,1,0:T(8,128)}, u32[]{:S(2)}) copy-start(f32[1,1,2,512,512]{4,3,2,1,0:T(8,128)} %param.10) | copy-start | bytes 6291460
  0.6 121.3 %copy-start.1 = (f32[1,1,2,512,512]{4,3,2,1,0:T(8,128)S(1)}, f32[1,1,2,512,512]{4,3,2,1,0:T(8,128)}, u32[]{:S(2)}) copy-start(f32[1,1,2,512,512]{4,3,2,1,0:T(8,128)} %param.11) | copy-start | bytes 6291460
  0.7 121.3 %copy-start.3 = (s32[1,16]{1,0:T(1,128)S(1)}, s32[1,16]{1,0:T(1,128)}, u32[]{:S(2)}) copy-start(s32[1,16]{1,0:T(1,128)} %own_ref.3) | copy-start | bytes 196
  0.7 121.3 %copy-start.4 = (s32[1,16]{1,0:T(1,128)S(1)}, s32[1,16]{1,0:T(1,128)}, u32[]{:S(2)}) copy-start(s32[1,16]{1,0:T(1,128)} %slot_ref.3) | copy-start | bytes 196
  122.0 1.2 copy-start.2
  123.2 2.8 %copy-start.5 = (bf16[256,512]{1,0:T(8,128)(2,1)S(1)}, bf16[256,512]{1,0:T(8,128)(2,1)}, u32[]{:S(2)}) copy-start(bf16[256,512]{1,0:T(8,128)(2,1)} %get-tuple-element.14) | copy-start | bytes 786436

commit v4 on v3

--- a/solution.py
+++ b/solution.py
@@ -10,8 +10,9 @@
 N = 512
 HALF = 256
 Q = 128
-NZ, NY, NT = 8, 4, 8
+NZ, NY, NX, NT = 8, 4, 4, 8
 SLOTS, NBLK, TOK = 2, 16, 256
+XTOK = TOK // NX
 EXTRA = 16
 BETA = 0.95
 MESH = pl.DeviceIdType.MESH
@@ -64,13 +65,15 @@
 def step_kernel(
     a_ref, o_ref, own_ref, slot_ref, l_ref, r_ref, out_ref, h_ref,
     l_buf, r_buf, tp, got, t_snd, t_rcv, t_fin, t_all,
-    a_buf, ot_buf, snd, rcv, gath_0, gath_1, g_all, stage, xl_buf, pre_buf, sums,
+    a_buf, o_buf, ot_buf, snd, rcv, gath_0, gath_1, g_all, stage, xl_buf, pre_buf, sums,
     st_sem, t_send, t_recv, c_send, c_recv, ta_send, ta_recv,
-    o_send, o_recv, own_sem, a_send, a_recv, f_send, f_recv,
+    o_send, o_recv, own_sem, a_send, a_recv, x_send, x_recv, f_send, f_recv,
     r_send, r_recv, g_send, g_recv, ga_send, ga_recv, y_send, y_recv, s_send, s_recv,
 ):
     dp, t, z, y = place()
-    core = lax.rem(t, 2)
+    core, x = lax.rem(t, 2), t // 2
+    low = lax.rem(x, 2)
+    xt = [2 * lax.rem(x + i, NX) + core for i in (1, NX - 1)]
     gath = (gath_0, gath_1)
     twin = t + 1 - 2 * core
     ys = [lax.rem(y + j, NY) for j in range(NY)]
@@ -104,13 +107,13 @@
     def own_copy(k, p):
         c = chunk_of(z, k)
         return pltpu.make_async_copy(
-            a_ref.at[:, columns(c, p, y)], a_buf.at[c, p, 0], own_sem.at[k, p]
+            a_ref.at[:, :, :, columns(c, p, y)], a_buf.at[c, p, :, :, 0], own_sem.at[k, p]
         )
 
     for k in range(NZ):
         for p in range(2):
             own_copy(k, p).start()
-    ot_buf[0] = o_ref[...].T
+    o_buf[:, :, 0] = o_ref[...]
 
     row = lax.broadcasted_iota(jnp.int32, (N, N), 0)
     col = lax.broadcasted_iota(jnp.int32, (N, N), 1)
@@ -134,29 +137,39 @@
             t_copy(j, s, y).start()
 
     def o_copy(j):
-        return remote(ot_buf.at[0], ot_buf.at[j], o_send.at[j], o_recv.at[j], ydp[j], t)
+        return remote(o_ref, o_buf.at[:, :, j], o_send.at[j], o_recv.at[j], ydp[j], t)
 
     def a_copy(k, j):
         c = chunk_of(z, k)
         return remote(
-            a_ref.at[:, columns(c, core, ys[j])], a_buf.at[c, core, j],
+            a_ref.at[:, low, :, columns(c, core, ys[j])], a_buf.at[c, core, :, low, j],
             a_send.at[k, j], a_recv.at[k, j], ydp[j], t,
         )
 
+    def x_copy(k, i, parity):
+        part = a_buf.at[chunk_of(z, k), core, i, parity, 1:]
+        return remote(part, part, x_send.at[k, i], x_recv.at[k, i], dp, xt[i])
+
     def f_copy(k, p):
-        part = a_buf.at[chunk_of(z, k), p, 1:]
+        part = a_buf.at[chunk_of(z, k), p, :, :, 1:]
         return remote(part, part, f_send.at[k], f_recv.at[k], dp, twin)
 
-    def to_twin(k):
+    def along_x(k):
         for j in (1, 3, 2):
             a_copy(k, j).wait_recv()
+        for i in range(2):
+            x_copy(k, i, low).start()
+
+    def to_twin(k):
+        for i in range(2):
+            x_copy(k, i, 1 - low).wait_recv()
         f_copy(k, core).start()
 
-    for j in (2, 1, 3):
-        o_copy(j).start()
     for k in range(NZ):
         for j in (2, 1, 3):
             a_copy(k, j).start()
+    for j in (2, 1, 3):
+        o_copy(j).start()
     got[y] = tp[y]
 
     def t_chain(d, s, p):
@@ -180,6 +193,7 @@
                 value = jnp.where(oz == z, value, t_rcv[d, s - 1, p])
             t_snd[d, s, p] = value
             t_chain(d, s, p).start()
+        along_x(k)
     for p in range(2):
         oz, oy, os = place_of(z, p)
         for d in (RIGHT, LEFT):
@@ -207,17 +221,18 @@
 
     for j in (1, 3, 2):
         o_copy(j).wait_recv()
-    outs = jnp.concatenate([ot_buf[j] for j in range(NY)], axis=1)
     to_twin(0)
+    ot_buf[...] = o_buf[...].reshape(NY * TOK, N).T
+    to_twin(1)
     for k in range(NZ):
         c = chunk_of(z, k)
-        if k + 1 < NZ:
-            to_twin(k + 1)
+        if k + 2 < NZ:
+            to_twin(k + 2)
         for p in range(2):
             own_copy(k, p).wait()
         f_copy(k, 1 - core).wait_recv()
         acts = jnp.concatenate([a_buf[c, p].reshape(NY * TOK, Q) for p in range(2)], axis=1)
-        part = dot(outs, acts, 1, 0)
+        part = dot(ot_buf[...], acts, 1, 0)
         part = [part[:, :Q], part[:, Q:]]
         for d, s, p in moves_of(k):
             value = part[p]
@@ -335,8 +350,8 @@
     hop(2, 1)
     sum_start(1, sum_end(0))
     hop(3, 1)
+    to_owners(0)
     sum_start(2, sum_end(1))
-    to_owners(0)
     to_owners(1)
     total = sum_end(2)
     ratio = jnp.sqrt(total[0] / total[1])[0:1, 0:1]
@@ -357,6 +372,8 @@
             y_copy(j, y, i).wait_send()
     for k in range(NZ):
         f_copy(k, core).wait_send()
+        for i in range(2):
+            x_copy(k, i, low).wait_send()
         for j in (1, 2, 3):
             a_copy(k, j).wait_send()
         for d, s, p in moves_of(k):
@@ -425,8 +442,9 @@
             pltpu.VMEM((2, 4, 2, N + EXTRA, Q), bf16),
             pltpu.VMEM((2, N + EXTRA, Q), bf16),
             pltpu.VMEM((NY, N + EXTRA, Q), bf16),
-            pltpu.VMEM((NZ, 2, NY, TOK, Q), bf16),
-            pltpu.VMEM((NY, N, TOK), bf16),
+            pltpu.VMEM((NZ, 2, 2, 2, NY, XTOK, Q), bf16),
+            pltpu.VMEM((2, 2, NY, XTOK, N), bf16),
+            pltpu.VMEM((N, NY * TOK), bf16),
             pltpu.VMEM((2, 4, 2, N, Q), bf16),
             pltpu.VMEM((2, 4, 2, N, Q), bf16),
             pltpu.VMEM((NBLK, HALF, Q), bf16),
@@ -443,6 +461,7 @@
             DMA((NY,)), DMA((NY,)),
             DMA((NZ, 2)),
             DMA((NZ, NY)), DMA((NZ, NY)),
+            DMA((NZ, 2)), DMA((NZ, 2)),
             DMA((NZ,)), DMA((NZ,)),
             DMA((2, 4, 2)), DMA((2, 4, 2)),
             DMA((2, 4, 2, 2)), DMA((2, 4, 2, 2)),
@@ -455,7 +474,7 @@
         ),
         name="step",
     )(
-        activations, out_grads, owner, slot,
+        activations.reshape(2, 2, XTOK, -1), out_grads.reshape(2, 2, XTOK, N), owner, slot,
         left_state[0, 0], right_state[0, 0],
     )
     state = pl.BlockSpec((1, N, N), lambda s: (s, 0, 0))

time: 127 us -> 124 us (0.976)
  Pallas kernels: 124 us -> 122 us
    pallas_call x1, Pallas kernels: 121 us -> 118 us  [shards(): pl.pallas_call(step_kernel, out_shape=[jax.ShapeDtypeStruct((TOK, N), bf1...]
where the time goes in v4:
time: 124 us
  Pallas kernels  122 us (98%)
  local copies, waits for them, and re-layouts  1.94 us (2%)
    pallas_call x1, Pallas kernels, shards(): pl.pallas_call(step_kernel, out_shape=[jax.ShapeDtypeStruct((TOK, N), bf1...  118 us
    pallas_call x1, Pallas kernels, shards(): pl.pallas_call(update_kernel, grid=(SLOTS,), out_shape=[jax.ShapeDtypeStr...  3.39 us

profile of v4, /device:TPU:1, one launch (start us, length us, event | category | flops | bytes accessed | tf_op | source)
XLA Modules:
  0.0 124.2 jit_solution(1906190408190772438)
XLA Ops:
  0.6 0.0 copy-start
  0.6 0.0 copy-start.1
  0.7 0.0 copy-start.3
  0.7 0.0 copy-start.4
  0.7 118.2 %step.1 = (bf16[256,512]{1,0:T(8,128)(2,1)}, bf16[2,4,2,256,128]{4,3,2,1,0:T(8,128)(2,1)}) custom-call(bf16[2,2,64,8192]{3,2,1,0:T(8,128)(2,1)} %bitcast.10, bf16[2,2,64,512]{3,2,1,0:T(8,128)(2,1)} %bitcast.11, s32[1,16]{1,0:T(1,128)} %own_ref.3, s32[1,16]{1,0:T(1,128)} %slot_ref.3, f32[2,512,512]{2,1,0:T(8,128)} %bitcast.6, f32[2,512,512]{2,1,0:T(8,128)} %bitcast.8), custom_call_target="tpu_custom_call" | custom-call | tf_op jit(solution)/shard_map/step/pallas_call | solution.py:428
  118.8 0.0 copy-done
  118.9 0.0 copy-done.1
  118.9 0.0 copy-done.3
  118.9 0.0 copy-done.4
  118.9 0.0 copy-start.2
  118.9 1.2 copy-done.2
  120.1 0.0 copy-start.5
  120.1 3.4 %update.1 = (f32[2,512,512]{2,1,0:T(8,128)}, f32[2,512,512]{2,1,0:T(8,128)}) custom-call(s32[1,16]{1,0:T(1,128)S(1)} %copy-done.3, s32[1,16]{1,0:T(1,128)S(1)} %copy-done.4, bf16[2,4,2,256,128]{4,3,2,1,0:T(8,128)(2,1)S(1)} %copy-done.2, f32[2,512,512]{2,1,0:T(8,128)S(1)} %bitcast.7, f32[2,512,512]{2,1,0:T(8,128)S(1)} %bitcast.9), custom_call_target="tpu_custom_call" | custom-call | tf_op jit(solution)/shard_map/update/pallas_call | solution.py:481
  123.5 0.0 copy-done.5
  123.5 0.7 copy.10
Async XLA Ops:
  0.6 118.2 %copy-start = (f32[1,1,2,512,512]{4,3,2,1,0:T(8,128)S(1)}, f32[1,1,2,512,512]{4,3,2,1,0:T(8,128)}, u32[]{:S(2)}) copy-start(f32[1,1,2,512,512]{4,3,2,1,0:T(8,128)} %param.10) | copy-start | bytes 6291460
  0.6 118.2 %copy-start.1 = (f32[1,1,2,512,512]{4,3,2,1,0:T(8,128)S(1)}, f32[1,1,2,512,512]{4,3,2,1,0:T(8,128)}, u32[]{:S(2)}) copy-start(f32[1,1,2,512,512]{4,3,2,1,0:T(8,128)} %param.11) | copy-start | bytes 6291460
  0.7 118.2 %copy-start.3 = (s32[1,16]{1,0:T(1,128)S(1)}, s32[1,16]{1,0:T(1,128)}, u32[]{:S(2)}) copy-start(s32[1,16]{1,0:T(1,128)} %own_ref.3) | copy-start | bytes 196
  0.7 118.2 %copy-start.4 = (s32[1,16]{1,0:T(1,128)S(1)}, s32[1,16]{1,0:T(1,128)}, u32[]{:S(2)}) copy-start(s32[1,16]{1,0:T(1,128)} %slot_ref.3) | copy-start | bytes 196
  118.9 1.2 copy-start.2
  120.1 3.4 %copy-start.5 = (bf16[256,512]{1,0:T(8,128)(2,1)S(1)}, bf16[256,512]{1,0:T(8,128)(2,1)}, u32[]{:S(2)}) copy-start(bf16[256,512]{1,0:T(8,128)(2,1)} %get-tuple-element.14) | copy-start | bytes 786436
